TPU v7x, 32 devices: a whole 2x2x4 slice. The times are simulated.
32 devices in a mesh: groups: 2 (over y), expert: 16 (over z, x, core), tensor: 1.
Axes of the slice: x: 2, y: 2, z: 4, core: 2. Of those that a mesh axis runs over, the one named last changes fastest.
Arguments:
- tokens_one: bfloat16 [1024, 2048], P(('groups', 'expert', 'tensor')), parts along dimension 0, may hold values from -6 to 6
- tokens_two: bfloat16 [1024, 2048], P(('groups', 'expert', 'tensor')), parts along dimension 0, may hold values from -6 to 6
- experts_one: int32 [1024, 8], P(('groups', 'expert')), parts along dimension 0, may hold values from 0 to 15, all different within a row; in each aligned block of 32 rows (0 to 31, 32 to 63, ...) at most 24 rows name the same one
- experts_two: int32 [1024, 8], P(('groups', 'expert')), parts along dimension 0, may hold values from 0 to 15, all different within a row; in each aligned block of 32 rows (0 to 31, 32 to 63, ...) at most 24 rows name the same one
- gates_one: float32 [1024, 8], P(('groups', 'expert')), parts along dimension 0, may hold values from 0.02 to 1
- gates_two: float32 [1024, 8], P(('groups', 'expert')), parts along dimension 0, may hold values from 0.02 to 1
- old_placement: int32 [16], replicated, may hold values from 0 to 15, each once
- swap_flags: int32 [8], replicated, may hold values 0 or 1
- gate_up: bfloat16 [16, 2048, 2, 768], P('expert', None, None, 'tensor'), may hold values from -0.125 to 0.125
- down: bfloat16 [16, 768, 2048], P('expert', 'tensor'), may hold values from -0.21875 to 0.21875
Outputs:
- out_one: bfloat16 [1024, 2048], P(('groups', 'expert', 'tensor')), parts along dimension 0
- out_two: bfloat16 [1024, 2048], P(('groups', 'expert', 'tensor')), parts along dimension 0
- new_gate_up: bfloat16 [32, 2048, 2, 768], P(('groups', 'expert'), None, None, 'tensor'), parts along dimension 0
- new_down: bfloat16 [32, 768, 2048], P(('groups', 'expert'), 'tensor'), parts along dimension 0
There are 2 independent parts, one for each index of `groups`. A program takes and returns all parts, laid end to end along the dimension named above; an argument that names none is the same for every part. Nothing has to cross between parts.
Inputs may be any that keep to these rules, and one draw needn't show every extreme that they name: `experts_one`: the ids of one row differ. In each aligned block of 32 rows no expert is named by more than 24 rows, a bound that some block reaches. `experts_two`: the ids of one row differ. In each aligned block of 32 rows no expert is named by more than 24 rows, a bound that some block reaches. `old_placement`: each expert appears once. `swap_flags`: entry p refers to the slots p and p + 8.
All inputs are finite; a program needn't handle non-finite values.
Results may differ from a plain program's by a relative error of at most 0.0058.
Values may be sent and summed in bfloat16 or wider, within the bound.
No kernel may reach another device: no remote copies, remote signals or barrier semaphores. Data moves between devices by JAX's collectives and lax.ppermute only.
A program may use at most 128 MiB of HBM per device.

v0:
```python
import jax
import jax.numpy as jnp
from jax import lax
from jax.sharding import PartitionSpec as P


def swapped(value, axis, bit):
    mask = 2**bit
    pairs = [(source, source ^ mask) for source in range(lax.axis_size(axis))]
    return lax.ppermute(value, axis, pairs)


def slot_table(placement, slot_index):
    match_table = placement[:, None] == slot_index[None, :]
    return jnp.sum(jnp.where(match_table, slot_index[:, None], 0), axis=0)


def expert_ffn(received, gate_up_w, down_w):
    peer_count = received.shape[0]
    item_count = received.shape[1]
    width = received.shape[2]
    half_width = down_w.shape[1]
    flat_rows = received.reshape(peer_count * item_count, width)
    projected = jnp.dot(
        flat_rows, gate_up_w[0].reshape(width, 2 * half_width), preferred_element_type=jnp.float32
    )
    hidden = (jax.nn.silu(projected[:, :half_width]) * projected[:, half_width:]).astype(
        jnp.bfloat16
    )
    output_rows = jnp.dot(hidden, down_w[0], preferred_element_type=jnp.float32).astype(
        jnp.bfloat16
    )
    return output_rows.reshape(peer_count, item_count, width)


def expert_layer(pair_rows, chosen, gates, slot_of, gate_up_w, down_w):
    row_total = pair_rows.shape[0]
    width = pair_rows.shape[1]
    top_count = chosen.shape[1]
    peer_total = lax.axis_size("expert")
    capacity = min(row_total, max(2, 3 * row_total * top_count // (2 * peer_total)))
    norm_gates = gates / jnp.sum(gates, axis=-1, keepdims=True)
    slot_index = jnp.arange(peer_total, dtype=jnp.int32)
    flat_ids = chosen.reshape(-1)
    expert_hot = flat_ids[:, None] == slot_index[None, :]
    target = jnp.sum(jnp.where(expert_hot, slot_of[None, :], 0), axis=1)
    target_hot = target[:, None] == slot_index[None, :]
    running = jnp.cumsum(target_hot.astype(jnp.int32), axis=0)
    position = jnp.sum(jnp.where(target_hot, running, 0), axis=1) - 1
    outgoing = jnp.zeros((peer_total, capacity, width), jnp.bfloat16)
    outgoing = outgoing.at[target, position].set(jnp.repeat(pair_rows, top_count, axis=0))
    received = lax.all_to_all(outgoing, "expert", split_axis=0, concat_axis=0, tiled=True)
    returned = lax.all_to_all(
        expert_ffn(received, gate_up_w, down_w), "expert", split_axis=0, concat_axis=0, tiled=True
    )
    picked = returned[target, position].astype(jnp.float32)
    weighted = picked * norm_gates.reshape(-1)[:, None]
    partial_value = jnp.sum(weighted.reshape(row_total, top_count, width), axis=1)
    return lax.psum_scatter(partial_value, "tensor", scatter_dimension=0, tiled=True).astype(
        jnp.bfloat16
    )


def body(
    tokens_one,
    tokens_two,
    experts_one,
    experts_two,
    gates_one,
    gates_two,
    old_placement,
    swap_flags,
    gate_up,
    down,
):
    peer_total = lax.axis_size("expert")
    half_count = peer_total // 2
    own_index = lax.axis_index("expert")
    slot_index = jnp.arange(peer_total, dtype=jnp.int32)
    partner = (slot_index + half_count) % peer_total
    swap_slots = swap_flags[slot_index % half_count] == 1
    new_placement = jnp.where(swap_slots, old_placement[partner], old_placement)
    pair_one, pair_two = (
        lax.all_gather(tokens_one, "tensor", axis=0, tiled=True),
        lax.all_gather(tokens_two, "tensor", axis=0, tiled=True),
    )
    half_bit = half_count.bit_length() - 1
    partner_gate_up, partner_down = swapped((gate_up, down), "expert", half_bit)
    swap_here = swap_flags[own_index % half_count] == 1
    new_gate_up = jnp.where(swap_here, partner_gate_up, gate_up)
    new_down = jnp.where(swap_here, partner_down, down)
    old_slots = slot_table(old_placement, slot_index)
    out_one = expert_layer(pair_one, experts_one, gates_one, old_slots, gate_up, down)
    out_two = expert_layer(
        pair_two,
        experts_two,
        gates_two,
        slot_table(new_placement, slot_index),
        new_gate_up,
        new_down,
    )
    return (out_one, out_two, new_gate_up, new_down)


def solution(mesh):
    return jax.shard_map(
        body,
        mesh=mesh,
        in_specs=(
            P(("groups", "expert", "tensor"), None),
            P(("groups", "expert", "tensor"), None),
            P(("groups", "expert"), None),
            P(("groups", "expert"), None),
            P(("groups", "expert"), None),
            P(("groups", "expert"), None),
            P(),
            P(),
            P("expert", None, None, "tensor"),
            P("expert", "tensor", None),
        ),
        out_specs=(
            P(("groups", "expert", "tensor"), None),
            P(("groups", "expert", "tensor"), None),
            P(("groups", "expert"), None, None, "tensor"),
            P(("groups", "expert"), "tensor", None),
        ),
        check_vma=False,
    )
```

profile of v0, /device:TPU:8, one launch (start us, length us, event | category | flops | bytes accessed | tf_op | source)
XLA Modules:
  0.0 612.7 jit_solution(9116034657239291208)
XLA Ops:
  0.6 0.0 copy-start
  0.6 0.8 copy.22
  1.4 0.1 eq.116
  1.5 0.7 select_reduce_fusion.3
  2.3 0.1 select_reduce_fusion.1
  2.4 0.6 reduce-window.14
  3.0 0.2 slice_reduce_fusion.1
  3.2 0.1 fusion.21
  3.3 0.0 copy-done
  3.3 0.1 broadcast_bitcast_fusion.1
  3.5 1.3 broadcast.244.clone
  4.8 44.4 %scatter_fusion = bf16[16,24,2048]{2,1,0:T(8,128)(2,1)} fusion(bf16[16,24,2048]{2,1,0:T(8,128)(2,1)} %broadcast.244.clone, s32[256]{0:T(256)S(1)} %bitcast.91, bf16[256,2048]{1,0:T(8,128)(2,1)S(1)} %broadcast_bitcast_fusion.1), kind=kCustom, calls=%fused_computation.4 | custom fusion | bytes 3147776 | tf_op jit(solution)/shard_map/scatter | solution.py:51
  49.2 0.0 copy-start.9
  49.2 0.0 copy-start.1
  49.2 0.0 copy-start.2
  49.2 6.4 %all-to-all-start = ((bf16[16,24,2048]{2,1,0:T(8,128)(2,1)}), bf16[16,24,2048]{2,1,0:T(8,128)(2,1)S(1)}, u32[]{:S(2)}, u32[]{:S(2)}) async-start(bf16[16,24,2048]{2,1,0:T(8,128)(2,1)} %scatter_fusion), calls=%async_computation | async-start | bytes 3145728 | tf_op jit(solution)/shard_map/all_to_all | solution.py:52
  55.6 2.4 collective-permute-start
  58.0 0.0 copy-done.9
  58.0 0.1 copy.25
  58.1 0.1 eq.130
  58.2 0.0 copy-done.1
  58.2 0.7 gather_fusion.2
  58.9 0.0 copy-done.2
  58.9 0.7 gather_fusion.1
  59.5 0.1 select_reduce_fusion.2
  59.6 0.1 select_reduce_fusion
  59.7 0.6 reduce-window.16
  60.3 0.2 slice_reduce_fusion
  60.5 0.1 fusion.19
  60.7 0.0 copy-done.6
  60.7 0.1 broadcast_bitcast_fusion
  60.8 1.3 broadcast.244.clone.1
  62.2 44.4 %scatter_fusion.1 = bf16[16,24,2048]{2,1,0:T(8,128)(2,1)} fusion(bf16[16,24,2048]{2,1,0:T(8,128)(2,1)} %broadcast.244.clone.1, s32[256]{0:T(256)S(1)} %bitcast.90, bf16[256,2048]{1,0:T(8,128)(2,1)S(1)} %broadcast_bitcast_fusion), kind=kCustom, calls=%fused_computation.5 | custom fusion | bytes 3147776 | tf_op jit(solution)/shard_map/scatter | solution.py:51
  106.5 119.0 %all-to-all-done = bf16[16,24,2048]{2,1,0:T(8,128)(2,1)S(1)} async-done(((bf16[16,24,2048]{2,1,0:T(8,128)(2,1)}), bf16[16,24,2048]{2,1,0:T(8,128)(2,1)S(1)}, u32[]{:S(2)}, u32[]{:S(2)}) %all-to-all-start) | async-done | bytes 1572896 | tf_op jit(solution)/shard_map/all_to_all | solution.py:52
  225.6 1.1 copy-done.4
  226.7 6.4 %all-to-all-start.2 = ((bf16[16,24,2048]{2,1,0:T(8,128)(2,1)}), bf16[16,24,2048]{2,1,0:T(8,128)(2,1)S(1)}, u32[]{:S(2)}, u32[]{:S(2)}) async-start(bf16[16,24,2048]{2,1,0:T(8,128)(2,1)} %scatter_fusion.1), calls=%async_computation.2 | async-start | bytes 3145728 | tf_op jit(solution)/shard_map/all_to_all | solution.py:52
  233.0 2.4 collective-permute-start.1
  235.4 4.3 copy.30
  239.7 0.0 copy-done.5
  239.7 2.6 fusion.33
  242.3 4.5 fusion.4
  246.8 214.8 %all-to-all-done.2 = bf16[16,24,2048]{2,1,0:T(8,128)(2,1)S(1)} async-done(((bf16[16,24,2048]{2,1,0:T(8,128)(2,1)}), bf16[16,24,2048]{2,1,0:T(8,128)(2,1)S(1)}, u32[]{:S(2)}, u32[]{:S(2)}) %all-to-all-start.2) | async-done | bytes 1572896 | tf_op jit(solution)/shard_map/all_to_all | solution.py:52
  461.6 6.4 %all-to-all-start.1 = ((bf16[16,24,2048]{2,1,0:T(8,128)(2,1)}), bf16[16,24,2048]{2,1,0:T(8,128)(2,1)S(1)}, u32[]{:S(2)}, u32[]{:S(2)}) async-start(bf16[16,24,2048]{2,1,0:T(8,128)(2,1)} %bitcast.96), calls=%async_computation.1 | async-start | bytes 3145728 | tf_op jit(solution)/shard_map/all_to_all | solution.py:53
  467.9 0.6 dynamic_slice.3
  469.2 76.8 %collective-permute-done.1 = bf16[1,768,2048]{2,1,0:T(8,128)(2,1)} collective-permute-done((bf16[1,768,2048]{2,1,0:T(8,128)(2,1)}, bf16[1,768,2048]{2,1,0:T(8,128)(2,1)}, u32[]{:S(2)}, u32[]{:S(2)}) %collective-permute-start.1) | collective-permute-done | bytes 3145760 | tf_op jit(solution)/shard_map/ppermute | solution.py:10
  545.9 2.2 broadcast_select_fusion.1
  548.2 0.0 copy-start.3
  548.2 0.0 collective-permute-done
  548.2 7.3 %broadcast_select_fusion = bf16[1,512,8,768]{3,2,1,0:T(8,128)(2,1)} fusion(bf16[1,512,8,768]{3,2,1,0:T(8,128)(2,1)} %bitcast.81, bf16[1,512,8,768]{3,2,1,0:T(8,128)(2,1)} %bitcast.85, pred[]{:T(512)} %bitcast.22), kind=kLoop, calls=%fused_computation.6 | loop fusion | flops 3145728 | bytes 18874368 | tf_op jit(solution)/shard_map/jit(_where)/select_n | solution.py:90
  555.4 4.1 copy.31
  559.6 2.6 fusion.34
  562.2 0.0 copy-done.3
  562.2 2.6 fusion.7
  564.8 0.0 all-to-all-done.1
  564.8 7.1 %all-to-all-start.3 = ((bf16[16,24,2048]{2,1,0:T(8,128)(2,1)}), bf16[16,24,2048]{2,1,0:T(8,128)(2,1)S(1)}, u32[]{:S(2)}, u32[]{:S(2)}) async-start(bf16[16,24,2048]{2,1,0:T(8,128)(2,1)} %bitcast.97), calls=%async_computation.3 | async-start | bytes 3145728 | tf_op jit(solution)/shard_map/all_to_all | solution.py:53
  571.9 0.0 copy-done.7
  571.9 0.1 copy.27
  572.0 0.0 copy-done.8
  572.0 0.1 copy.24
  572.1 5.3 gather_fusion
  577.4 2.9 fusion.11
  580.3 26.5 %all-to-all-done.3 = bf16[16,24,2048]{2,1,0:T(8,128)(2,1)S(1)} async-done(((bf16[16,24,2048]{2,1,0:T(8,128)(2,1)}), bf16[16,24,2048]{2,1,0:T(8,128)(2,1)S(1)}, u32[]{:S(2)}, u32[]{:S(2)}) %all-to-all-start.3) | async-done | bytes 1572896 | tf_op jit(solution)/shard_map/all_to_all | solution.py:53
  606.7 4.3 gather_fusion.3
  611.0 1.6 fusion.10
  (24 shorter events, 0.2 us)
Async XLA Ops:
  0.6 2.7 copy-start
  49.2 8.8 %copy-start.9 = (s32[32,8]{0,1:T(8,128)S(1)}, s32[32,8]{0,1:T(8,128)}, u32[]{:S(2)}) copy-start(s32[32,8]{0,1:T(8,128)} %param.13) | copy-start | bytes 3076
  49.2 9.0 %copy-start.1 = (s32[16]{0:T(128)S(1)}, s32[16]{0:T(128)}, u32[]{:S(2)}) copy-start(s32[16]{0:T(128)} %param.16) | copy-start | bytes 196
  49.2 9.7 %copy-start.2 = (s32[8]{0:T(128)S(1)}, s32[8]{0:T(128)}, u32[]{:S(2)}) copy-start(s32[8]{0:T(128)} %param.17) | copy-start | bytes 100
  49.2 11.4 %copy-start.6 = (bf16[32,2048]{1,0:T(8,128)(2,1)S(1)}, bf16[32,2048]{1,0:T(8,128)(2,1)}, u32[]{:S(2)}) copy-start(bf16[32,2048]{1,0:T(8,128)(2,1)} %param.11) | copy-start | bytes 393220
  49.2 176.3 %all-to-all-start = ((bf16[16,24,2048]{2,1,0:T(8,128)(2,1)}), bf16[16,24,2048]{2,1,0:T(8,128)(2,1)S(1)}, u32[]{:S(2)}, u32[]{:S(2)}) async-start(bf16[16,24,2048]{2,1,0:T(8,128)(2,1)} %scatter_fusion), calls=%async_computation | async-start | bytes 3145728 | tf_op jit(solution)/shard_map/all_to_all | solution.py:52
  55.6 492.6 %collective-permute-start = (bf16[1,2048,2,768]{3,2,1,0:T(2,128)(2,1)}, bf16[1,2048,2,768]{3,2,1,0:T(2,128)(2,1)}, u32[]{:S(2)}, u32[]{:S(2)}) collective-permute-start(bf16[1,2048,2,768]{3,2,1,0:T(2,128)(2,1)} %param.18), channel_id=1, source_target_pairs={{0,8},{1,9},{2,10},{3,11},{4,12},{5,13},{6,14},{7,15},{8,0},{9,1},... | collective-permute-start | bytes 18874376 | tf_op jit(solution)/shard_map/ppermute | solution.py:10
  225.5 1.1 copy-start.4
  226.7 234.9 %all-to-all-start.2 = ((bf16[16,24,2048]{2,1,0:T(8,128)(2,1)}), bf16[16,24,2048]{2,1,0:T(8,128)(2,1)S(1)}, u32[]{:S(2)}, u32[]{:S(2)}) async-start(bf16[16,24,2048]{2,1,0:T(8,128)(2,1)} %scatter_fusion.1), calls=%async_computation.2 | async-start | bytes 3145728 | tf_op jit(solution)/shard_map/all_to_all | solution.py:52
  233.0 312.9 %collective-permute-start.1 = (bf16[1,768,2048]{2,1,0:T(8,128)(2,1)}, bf16[1,768,2048]{2,1,0:T(8,128)(2,1)}, u32[]{:S(2)}, u32[]{:S(2)}) collective-permute-start(bf16[1,768,2048]{2,1,0:T(8,128)(2,1)} %param.19), channel_id=1, source_target_pairs={{0,8},{1,9},{2,10},{3,11},{4,12},{5,13},{6,14},{7,15},{8,0},{9,1},... | collective-permute-start | bytes 9437192 | tf_op jit(solution)/shard_map/ppermute | solution.py:10
  235.4 4.3 copy-start.5
  461.6 103.2 %all-to-all-start.1 = ((bf16[16,24,2048]{2,1,0:T(8,128)(2,1)}), bf16[16,24,2048]{2,1,0:T(8,128)(2,1)S(1)}, u32[]{:S(2)}, u32[]{:S(2)}) async-start(bf16[16,24,2048]{2,1,0:T(8,128)(2,1)} %bitcast.96), calls=%async_computation.1 | async-start | bytes 3145728 | tf_op jit(solution)/shard_map/all_to_all | solution.py:53
  548.2 14.1 %copy-start.3 = (bf16[1,768,2048]{2,1,0:T(8,128)(2,1)}, bf16[1,768,2048]{2,1,0:T(8,128)(2,1)S(1)}, u32[]{:S(2)}) copy-start(bf16[1,768,2048]{2,1,0:T(8,128)(2,1)S(1)} %broadcast_select_fusion.1) | copy-start | bytes 9437188
  564.8 7.1 %copy-start.7 = (f32[32,8]{0,1:T(8,128)S(1)}, f32[32,8]{0,1:T(8,128)}, u32[]{:S(2)}) copy-start(f32[32,8]{0,1:T(8,128)} %param.15) | copy-start | bytes 3076
  564.8 7.2 %copy-start.8 = (f32[32,8]{0,1:T(8,128)S(1)}, f32[32,8]{0,1:T(8,128)}, u32[]{:S(2)}) copy-start(f32[32,8]{0,1:T(8,128)} %param.14) | copy-start | bytes 3076
  564.8 41.9 %all-to-all-start.3 = ((bf16[16,24,2048]{2,1,0:T(8,128)(2,1)}), bf16[16,24,2048]{2,1,0:T(8,128)(2,1)S(1)}, u32[]{:S(2)}, u32[]{:S(2)}) async-start(bf16[16,24,2048]{2,1,0:T(8,128)(2,1)} %bitcast.97), calls=%async_computation.3 | async-start | bytes 3145728 | tf_op jit(solution)/shard_map/all_to_all | solution.py:53
where the time goes:
time: 618 us; the launch traced here: 613 us
  waiting for transfers between devices  437 us (71%)
  local copies, waits for them, and re-layouts  114 us (18%)
  starting transfers between devices  30.9 us (5%)
  other arithmetic  16.5 us (3%)
  matrix products  12.3 us (2%)
    all_to_all x2, waiting for transfers between devices, expert_layer(): lax.all_to_all(outgoing, 'expert', split_axis=0, concat_axis=0, tiled=True)  334 us
    scatter x2, local copies, waits for them, and re-layouts, expert_layer(): outgoing.at[target, position].set(jnp.repeat(pair_rows, top_count, axis=0))  88.8 us
    ppermute x2, waiting for transfers between devices, swapped(): return lax.ppermute(value, axis, pairs)  76.8 us
    all_to_all x2, waiting for transfers between devices, expert_layer(): lax.all_to_all(expert_ffn(received, gate_up_w, down_w), 'expert', split_a...  26.5 us
    all_to_all x2, starting transfers between devices, expert_layer(): lax.all_to_all(expert_ffn(received, gate_up_w, down_w), 'expert', split_a...  13.4 us
    all_to_all x2, starting transfers between devices, expert_layer(): lax.all_to_all(outgoing, 'expert', split_axis=0, concat_axis=0, tiled=True)  12.7 us
  transfers between devices with their start and end apart: 6, of which 4 were waited for; matrix products, arithmetic and copies ran while one was open for 14% of the time, Pallas kernels for 0%

commit v1 on v0

v1 whole, which is shorter than its diff:
```python
import jax
import jax.numpy as jnp
from jax import lax
from jax.sharding import PartitionSpec as P

LANES = 128


def xor_pairs(count, mask):
    return [(source, source ^ mask) for source in range(count)]


def shift_pairs(count, shift):
    return [(source, (source + shift) % count) for source in range(count)]


def exchange(value, mask):
    return lax.ppermute(value, "expert", xor_pairs(lax.axis_size("expert"), mask))


def slot_table(placement, slot_index):
    match_table = placement[:, None] == slot_index[None, :]
    return jnp.sum(jnp.where(match_table, slot_index[:, None], 0), axis=0)


def expert_ffn(rows, joined_w, down_w):
    half_width = down_w.shape[0]
    projected = jnp.dot(rows, joined_w, preferred_element_type=jnp.float32)
    hidden = (jax.nn.silu(projected[:, :half_width]) * projected[:, half_width:]).astype(
        jnp.bfloat16
    )
    return jnp.dot(hidden, down_w, preferred_element_type=jnp.float32)


def routed_layer(pair_rows, chosen, gates, slot_of, joined_w, down_w):
    row_total = pair_rows.shape[0]
    width = pair_rows.shape[1]
    top_count = chosen.shape[1]
    peer_total = lax.axis_size("expert")
    capacity = min(row_total, max(2, 3 * row_total * top_count // (2 * peer_total)))
    norm_gates = gates / jnp.sum(gates, axis=-1, keepdims=True)
    slot_index = jnp.arange(peer_total, dtype=jnp.int32)
    flat_ids = chosen.reshape(-1)
    expert_hot = flat_ids[:, None] == slot_index[None, :]
    target = jnp.sum(jnp.where(expert_hot, slot_of[None, :], 0), axis=1)
    target_hot = target[:, None] == slot_index[None, :]
    running = jnp.cumsum(target_hot.astype(jnp.int32), axis=0)
    position = jnp.sum(jnp.where(target_hot, running, 0), axis=1) - 1
    outgoing = jnp.zeros((peer_total, capacity, width), jnp.bfloat16)
    outgoing = outgoing.at[target, position].set(jnp.repeat(pair_rows, top_count, axis=0))
    received = lax.all_to_all(outgoing, "expert", split_axis=0, concat_axis=0, tiled=True)
    partial_rows = expert_ffn(received.reshape(-1, width), joined_w, down_w).astype(jnp.bfloat16)
    returned = lax.all_to_all(
        partial_rows.reshape(received.shape), "expert", split_axis=0, concat_axis=0, tiled=True
    )
    picked = returned[target, position].astype(jnp.float32)
    weighted = picked * norm_gates.reshape(-1)[:, None]
    partial_value = jnp.sum(weighted.reshape(row_total, top_count, width), axis=1)
    return lax.psum_scatter(partial_value, "tensor", scatter_dimension=0, tiled=True).astype(
        jnp.bfloat16
    )


def extended_rows(rows, chosen, gates, placement):
    norm_gates = gates / jnp.sum(gates, axis=-1, keepdims=True)
    hot = chosen[:, :, None] == placement[None, None, :]
    dense = jnp.sum(jnp.where(hot, norm_gates[:, :, None], 0.0), axis=1)
    high = lax.reduce_precision(dense, 8, 7)
    middle = lax.reduce_precision(dense - high, 8, 7)
    low = dense - high - middle
    slots = placement.shape[0]
    spare = jnp.zeros((rows.shape[0], LANES - 3 * slots), jnp.bfloat16)
    parts = [part.astype(jnp.bfloat16) for part in (high, middle, low)]
    return jnp.concatenate([rows, *parts, spare], axis=1)


def weighted_ffn(piece, width, slots, joined_w, down_w):
    own_index = lax.axis_index("expert")
    tail = piece[:, width:].astype(jnp.float32)
    column = lax.broadcasted_iota(jnp.int32, tail.shape, 1)
    mine = (column % slots == own_index) & (column < 3 * slots)
    weight = jnp.sum(jnp.where(mine, tail, 0.0), axis=1, keepdims=True)
    return weight * expert_ffn(piece[:, :width], joined_w, down_w)


def half_piece(array, axis, half, index, count):
    rows = array.shape[axis] // (2 * count)
    return lax.dynamic_slice_in_dim(array, (half * count + index) * rows, rows, axis=axis)


def assemble(shape, axis, group, own_parts, other_parts):
    result = jnp.zeros(shape, jnp.bfloat16)
    count = len(own_parts)
    rows = shape[axis] // (2 * count)
    for parts, half in ((own_parts, group), (other_parts, 1 - group)):
        for index, part in enumerate(parts):
            start = (half * count + index) * rows
            result = lax.dynamic_update_slice_in_dim(result, part, start, axis=axis)
    return result


def swap_steps(on, group, gate_up, down, plan):
    half_bit = lax.axis_size("expert") // 2
    counts = (
        sum(1 for step in plan for name, _ in step if name == "g"),
        sum(1 for step in plan for name, _ in step if name == "d"),
    )
    arrived, relayed, pending = {}, {}, []

    def cut(item):
        name, index = item
        if name == "g":
            return half_piece(gate_up, 1, group, index, counts[0])
        return half_piece(down, 1, group, index, counts[1])

    def step(items, work):
        nonlocal pending
        outgoing = [cut(item) for item in items]
        to_relay = [arrived[item] for item in pending]

        def active(args):
            outgoing, to_relay = args
            crossed = [exchange(value, half_bit) for value in outgoing]
            handed = [lax.ppermute(value, "groups", [(0, 1), (1, 0)]) for value in to_relay]
            return crossed, handed, work()

        def idle(args):
            outgoing, to_relay = args
            return list(outgoing), list(to_relay), work()

        crossed, handed, made = lax.cond(on, active, idle, (outgoing, to_relay))
        for item, value in zip(pending, handed):
            relayed[item] = value
        for item, value in zip(items, crossed):
            arrived[item] = value
        pending = list(items)
        return made

    def finish():
        to_relay = [arrived[item] for item in pending]

        def active(to_relay):
            handed = [lax.ppermute(value, "groups", [(0, 1), (1, 0)]) for value in to_relay]
            for item, value in zip(pending, handed):
                relayed[item] = value
            whole = []
            for name, count, like in (("g", counts[0], gate_up), ("d", counts[1], down)):
                whole.append(
                    assemble(
                        like.shape,
                        1,
                        group,
                        [arrived[name, index] for index in range(count)],
                        [relayed[name, index] for index in range(count)],
                    )
                )
            return tuple(whole)

        return lax.cond(on, active, lambda _: (gate_up, down), to_relay)

    return step, finish


PLAN = (
    (("g", 0),),
    (("g", 1), ("d", 0)),
    (("g", 2),),
    (("g", 3), ("d", 1)),
)


def staged(
    tokens, chosen, gates, placement, gate_up, down, step, finish
):
    peers = lax.axis_size("expert")
    levels = peers // 4
    rows, width = tokens.shape
    own = extended_rows(tokens, chosen, gates, placement)

    joined = lambda: gate_up[0].reshape(width, -1)
    ffn = lambda piece, joined_w: weighted_ffn(piece, width, peers, joined_w, down[0])

    columns = [own] + [
        lax.ppermute(own, "expert", shift_pairs(peers, 4 * hop)) for hop in range(1, levels)
    ]
    joined_w = step(PLAN[0], joined)
    here = jnp.concatenate(columns, axis=0)
    across = exchange(here, 2)
    here_core = exchange(here, 1)
    part_here, part_here_core = step(
        PLAN[1], lambda: (ffn(here, joined_w), ffn(here_core, joined_w).astype(jnp.bfloat16))
    )
    across_core = exchange(across, 1)
    got_here = exchange(part_here_core, 1)
    part_across, part_across_core = step(
        PLAN[2],
        lambda: (ffn(across, joined_w), ffn(across_core, joined_w).astype(jnp.bfloat16)),
    )
    got_across = exchange(part_across_core, 1)
    sum_across = (part_across + got_across.astype(jnp.float32)).astype(jnp.bfloat16)
    got_column = exchange(sum_across, 2)
    sum_here = step(PLAN[3], lambda: part_here + got_here.astype(jnp.float32))
    column = sum_here + got_column.astype(jnp.float32)
    total = column[:rows]
    returned = [
        lax.ppermute(
            column[hop * rows : (hop + 1) * rows].astype(jnp.bfloat16),
            "expert",
            shift_pairs(peers, peers - 4 * hop),
        )
        for hop in range(1, levels)
    ]
    new_gate_up, new_down = finish()
    for value in returned:
        total = total + value.astype(jnp.float32)
    total = total.astype(jnp.bfloat16)
    return total, new_gate_up, new_down


def body(
    tokens_one,
    tokens_two,
    experts_one,
    experts_two,
    gates_one,
    gates_two,
    old_placement,
    swap_flags,
    gate_up,
    down,
):
    peer_total = lax.axis_size("expert")
    half_count = peer_total // 2
    own_index = lax.axis_index("expert")
    group = lax.axis_index("groups")
    swap_here = swap_flags[own_index % half_count] == 1
    step, finish = swap_steps(swap_here, group, gate_up, down, PLAN)
    if lax.axis_size("tensor") == 1 and peer_total == 16:
        count = tokens_one.shape[0]
        total, new_gate_up, new_down = staged(
            jnp.concatenate([tokens_one, tokens_two], axis=0),
            jnp.concatenate([experts_one, experts_two], axis=0),
            jnp.concatenate([gates_one, gates_two], axis=0),
            old_placement,
            gate_up,
            down,
            step,
            finish,
        )
        return (total[:count], total[count:], new_gate_up, new_down)
    slot_index = jnp.arange(peer_total, dtype=jnp.int32)
    old_slots = slot_table(old_placement, slot_index)
    joined_w = gate_up[0].reshape(gate_up.shape[1], -1)
    outs = []
    for tokens, chosen, gates in (
        (tokens_one, experts_one, gates_one),
        (tokens_two, experts_two, gates_two),
    ):
        rows = lax.all_gather(tokens, "tensor", axis=0, tiled=True)
        outs.append(routed_layer(rows, chosen, gates, old_slots, joined_w, down[0]))
    for items in PLAN:
        step(items, lambda: ())
    new_gate_up, new_down = finish()
    return (outs[0], outs[1], new_gate_up, new_down)


def solution(mesh):
    return jax.shard_map(
        body,
        mesh=mesh,
        in_specs=(
            P(("groups", "expert", "tensor"), None),
            P(("groups", "expert", "tensor"), None),
            P(("groups", "expert"), None),
            P(("groups", "expert"), None),
            P(("groups", "expert"), None),
            P(("groups", "expert"), None),
            P(),
            P(),
            P("expert", None, None, "tensor"),
            P("expert", "tensor", None),
        ),
        out_specs=(
            P(("groups", "expert", "tensor"), None),
            P(("groups", "expert", "tensor"), None),
            P(("groups", "expert"), None, None, "tensor"),
            P(("groups", "expert"), "tensor", None),
        ),
        check_vma=False,
    )
```

time: 618 us -> 250 us (0.40)
  the two profiles are of different devices: /device:TPU:8 before, /device:TPU:11 now
where the time goes in v1:
time: 250 us; the launch traced here: 252 us
  waiting for transfers between devices  124 us (50%)
  local copies, waits for them, and re-layouts  61.9 us (25%)
  matrix products  29.6 us (12%)
  starting transfers between devices  26.4 us (11%)
  other arithmetic  8.78 us (4%)
    ppermute x12, waiting for transfers between devices, exchange(): lax.ppermute(value, 'expert', xor_pairs(lax.axis_size('expert'), mask))  99 us
    dynamic_update_slice x12, local copies, waits for them, and re-layouts, assemble(): result = lax.dynamic_update_slice_in_dim(result, part, start, axis=axis)  24.2 us
    ppermute x3, waiting for transfers between devices, staged(): lax.ppermute(own, 'expert', shift_pairs(peers, 4 * hop))  23.6 us
    unnamed x23, local copies, waits for them, and re-layouts  16.8 us
    dot_general x4, matrix products, expert_ffn(): projected = jnp.dot(rows, joined_w, preferred_element_type=jnp.float32)  15.8 us
    dot_general x4, matrix products, expert_ffn(): return jnp.dot(hidden, down_w, preferred_element_type=jnp.float32)  13.8 us
    ppermute x12, starting transfers between devices, exchange(): lax.ppermute(value, 'expert', xor_pairs(lax.axis_size('expert'), mask))  11.9 us
    dynamic_slice x5, local copies, waits for them, and re-layouts, half_piece(): lax.dynamic_slice_in_dim(array, (half * count + index) * rows, rows, axis...  9.23 us
  transfers between devices with their start and end apart: 24, of which 11 were waited for; matrix products, arithmetic and copies ran while one was open for 33% of the time, Pallas kernels for 0%

profile of v1, /device:TPU:11, one launch (start us, length us, event | category | flops | bytes accessed | tf_op | source)
XLA Modules:
  0.0 252.4 jit_solution(15935651281270854422)
XLA Ops:
  0.6 6.9 %copy.66 = bf16[1,2048,2,768]{3,2,1,0:T(2,128)(2,1)} copy(bf16[1,2048,2,768]{3,2,1,0:T(2,128)(2,1)} %param.28) | data formatting | bytes 12582912
  7.6 1.7 copy.67
  10.1 1.3 collective-permute-start.12
  11.5 1.1 collective-permute-start.13
  12.6 1.4 collective-permute-start.14
  13.9 3.7 %collective-permute-done.12 = bf16[64,2176]{1,0:T(8,128)(2,1)S(1)} collective-permute-done((bf16[64,2176]{1,0:T(8,128)(2,1)S(1)}, bf16[64,2176]{1,0:T(8,128)(2,1)S(1)}, u32[]{:S(2)}, u32[]{:S(2)}) %collective-permute-start.12) | collective-permute-done | bytes 278560 | tf_op jit(solution)/shard_map/ppermute | solution.py:184
  17.7 17.0 %collective-permute-done.13 = bf16[64,2176]{1,0:T(8,128)(2,1)S(1)} collective-permute-done((bf16[64,2176]{1,0:T(8,128)(2,1)S(1)}, bf16[64,2176]{1,0:T(8,128)(2,1)S(1)}, u32[]{:S(2)}, u32[]{:S(2)}) %collective-permute-start.13) | collective-permute-done | bytes 278560 | tf_op jit(solution)/shard_map/ppermute | solution.py:184
  34.7 2.8 %collective-permute-done.14 = bf16[64,2176]{1,0:T(8,128)(2,1)S(1)} collective-permute-done((bf16[64,2176]{1,0:T(8,128)(2,1)S(1)}, bf16[64,2176]{1,0:T(8,128)(2,1)S(1)}, u32[]{:S(2)}, u32[]{:S(2)}) %collective-permute-start.14) | collective-permute-done | bytes 278560 | tf_op jit(solution)/shard_map/ppermute | solution.py:184
  38.7 24.7 %collective-permute-done.15 = bf16[256,2176]{1,0:T(8,128)(2,1)} collective-permute-done((bf16[256,2176]{1,0:T(8,128)(2,1)S(1)}, bf16[256,2176]{1,0:T(8,128)(2,1)}, u32[]{:S(2)}, u32[]{:S(2)}) %collective-permute-start.15) | collective-permute-done | bytes 1114144 | tf_op jit(solution)/shard_map/ppermute | solution.py:18
  63.4 1.3 collective-permute-start.16
  66.0 19.3 %conditional.7 = (bf16[1,256,2,768]{3,2,1,0:T(2,128)(2,1)}, bf16[1,2048,2,768]{3,2,1,0:T(2,128)(2,1)}) conditional(s32[]{:T(128)} %bitcast.4, (bf16[1,2048,2,768]{3,2,1,0:T(2,128)(2,1)}, bf16[1,2048,2,768]{3,2,1,0:T(2,128)(2,1)}, s32[]{:T(128)}, s32[]{:T(128)}, s32[]{:T(128)}, /*index=5*/s32[]{:T(128)}, s32[]{:T(128)}, s32[]{:T(128)}) %tuple.57, ...), branch_computations={%region_2.3_spmd, %region_3.4_spmd} | conditional | flops 3 | bytes 4718686 | solution.py:131
  66.0 1.7 constant_dynamic-slice_fusion.1
  68.0 17.3 %collective-permute-done = bf16[1,256,2,768]{3,2,1,0:T(2,128)(2,1)} collective-permute-done((bf16[1,256,2,768]{3,2,1,0:T(2,128)(2,1)S(1)}, bf16[1,256,2,768]{3,2,1,0:T(2,128)(2,1)}, u32[]{:S(2)}, u32[]{:S(2)}) %collective-permute-start) | collective-permute-done | bytes 786464 | tf_op jit(solution)/shard_map/cond/branch_1_fun/ppermute | solution.py:18
  85.3 6.8 %copy.19 = bf16[256,8,2,768]{3,1,2,0:T(8,128)(2,1)} copy(bf16[256,8,2,768]{3,2,1,0:T(2,128)(2,1)} %bitcast.6) | data formatting | bytes 12582912
  92.1 2.4 constant_dynamic-slice_fusion.8
  94.5 1.2 constant_dynamic-slice_fusion.7
  95.8 36.2 %conditional.8 = (bf16[1,256,2,768]{3,2,1,0:T(2,128)(2,1)S(1)}, bf16[1,192,2048]{2,1,0:T(8,128)(2,1)S(1)}, bf16[1,256,2,768]{3,2,1,0:T(2,128)(2,1)}, f32[256,2048]{1,0:T(8,128)S(1)}, bf16[256,2048]{1,0:T(8,128)(2,1)}) conditional(s32[]{:T(128)} %bitcast.4, (bf16[256,2176]{1,0:T(8,128)(2,1)S(1)}, bf16[2048,1536]{1,0:T(8,128)(2,1)}, ...), branch_computations={%region_4.7_spmd, %region_7.10_spmd} | conditional | flops 4836065792 | bytes 68295384
  96.0 3.0 %collective-permute-start.6 = (bf16[1,256,2,768]{3,2,1,0:T(2,128)(2,1)S(1)}, bf16[1,256,2,768]{3,2,1,0:T(2,128)(2,1)}, u32[]{:S(2)}, u32[]{:S(2)}) collective-permute-start(bf16[1,256,2,768]{3,2,1,0:T(2,128)(2,1)S(1)} %get-tuple-element.138), channel_id=1, source_target_pairs={{0,8},{1,9},{2,10},{3,11},{4,12},{5,13},{6,14},{7,15},{8,0},{9,1},... | collective-permute-start | bytes 2359304 | tf_op jit(solution)/shard_map/cond/branch_1_fun/ppermute | solution.py:18
  99.0 1.2 collective-permute-start.8
  100.3 4.7 %fusion.35 = f32[256,1536]{1,0:T(8,128)S(1)} fusion(bf16[2048,1536]{1,0:T(8,128)(2,1)} %get-tuple-element.142, bf16[256,2176]{1,0:T(8,128)(2,1)S(1)} %get-tuple-element.141), kind=kOutput, calls=%fused_computation.36 | convolution fusion | flops 1610612736 | bytes 8912896 | tf_op jit(solution)/shard_map/cond/branch_1_fun/dot_general | solution.py:28
  105.0 3.0 %fusion.33 = f32[256,1536]{1,0:T(8,128)S(1)} fusion(bf16[2048,1536]{1,0:T(8,128)(2,1)S(1)} %copy-done.1, bf16[256,2176]{1,0:T(8,128)(2,1)} %get-tuple-element.144), kind=kOutput, calls=%fused_computation.34 | convolution fusion | flops 1610612736 | bytes 8912896 | tf_op jit(solution)/shard_map/cond/branch_1_fun/dot_general | solution.py:28
  109.0 3.0 %fusion.27 = f32[256,2048]{1,0:T(8,128)S(1)} fusion(bf16[1,768,2048]{2,1,0:T(8,128)(2,1)} %get-tuple-element.143, f32[256]{0:T(256)S(1)} %get-tuple-element.296, f32[256,1536]{1,0:T(8,128)S(1)} %fusion.35), kind=kOutput, calls=%fused_computation.32 | convolution fusion | flops 807010304 | bytes 6816768 | tf_op jit(solution)/shard_map/cond/branch_1_fun/dot_general | solution.py:32
  111.9 4.0 %fusion.30 = bf16[256,2048]{1,0:T(8,128)(2,1)} fusion(bf16[1,768,2048]{2,1,0:T(8,128)(2,1)} %get-tuple-element.143, f32[256]{0:T(256)S(1)} %get-tuple-element.295, f32[256,1536]{1,0:T(8,128)S(1)} %fusion.33), kind=kOutput, calls=%fused_computation.33 | convolution fusion | flops 807534592 | bytes 5768192 | tf_op jit(solution)/shard_map/cond/branch_1_fun/dot_general | solution.py:32
  115.9 6.5 %collective-permute-done.6 = bf16[1,256,2,768]{3,2,1,0:T(2,128)(2,1)} collective-permute-done((bf16[1,256,2,768]{3,2,1,0:T(2,128)(2,1)S(1)}, bf16[1,256,2,768]{3,2,1,0:T(2,128)(2,1)}, u32[]{:S(2)}, u32[]{:S(2)}) %collective-permute-start.6) | collective-permute-done | bytes 786464 | tf_op jit(solution)/shard_map/cond/branch_1_fun/ppermute | solution.py:18
  122.4 1.1 copy.39
  123.5 7.3 %collective-permute-done.7 = bf16[1,192,2048]{2,1,0:T(8,128)(2,1)} collective-permute-done((bf16[1,192,2048]{2,1,0:T(8,128)(2,1)S(1)}, bf16[1,192,2048]{2,1,0:T(8,128)(2,1)}, u32[]{:S(2)}, u32[]{:S(2)}) %collective-permute-start.7) | collective-permute-done | bytes 786464 | tf_op jit(solution)/shard_map/cond/branch_1_fun/ppermute | solution.py:18
  130.8 1.1 copy.40
  131.9 1.4 copy-done.5
  133.3 22.3 %conditional.9 = (bf16[1,256,2,768]{3,2,1,0:T(2,128)(2,1)S(1)}, bf16[1,256,2,768]{3,2,1,0:T(2,128)(2,1)}, bf16[1,192,2048]{2,1,0:T(8,128)(2,1)}, f32[256,2048]{1,0:T(8,128)S(1)}, bf16[256,2048]{1,0:T(8,128)(2,1)}) conditional(s32[]{:T(128)} %bitcast.4, (bf16[256,2176]{1,0:T(8,128)(2,1)}, bf16[2048,1536]{1,0:T(8,128)(2,1)}, ...), branch_computations={%region_10.13_spmd, %region_13.16_spmd} | conditional | flops 4836065792 | bytes 66722516
  133.3 2.9 %collective-permute-start.9 = (bf16[1,256,2,768]{3,2,1,0:T(2,128)(2,1)S(1)}, bf16[1,256,2,768]{3,2,1,0:T(2,128)(2,1)S(1)}, u32[]{:S(2)}, u32[]{:S(2)}) collective-permute-start(bf16[1,256,2,768]{3,2,1,0:T(2,128)(2,1)S(1)} %get-tuple-element.152), channel_id=1, source_target_pairs={{0,8},{1,9},{2,10},{3,11},{4,12},{5,13},{6,14},{7,15},{8,0},{9,1},... | collective-permute-start | bytes 2359304 | tf_op jit(solution)/shard_map/cond/branch_1_fun/ppermute | solution.py:18
  136.3 1.2 collective-permute-start.10
  137.7 5.0 %fusion.81 = f32[256,1536]{1,0:T(8,128)S(1)} fusion(bf16[2048,1536]{1,0:T(8,128)(2,1)} %get-tuple-element.156, bf16[256,2176]{1,0:T(8,128)(2,1)} %get-tuple-element.155), kind=kOutput, calls=%fused_computation.88 | convolution fusion | flops 1610612736 | bytes 8912896 | tf_op jit(solution)/shard_map/cond/branch_1_fun/dot_general | solution.py:28
  142.8 3.0 %fusion.79 = f32[256,1536]{1,0:T(8,128)S(1)} fusion(bf16[2048,1536]{1,0:T(8,128)(2,1)S(1)} %copy-done.3, bf16[256,2176]{1,0:T(8,128)(2,1)} %get-tuple-element.158), kind=kOutput, calls=%fused_computation.86 | convolution fusion | flops 1610612736 | bytes 8912896 | tf_op jit(solution)/shard_map/cond/branch_1_fun/dot_general | solution.py:28
  146.8 3.0 %fusion.73 = f32[256,2048]{1,0:T(8,128)S(1)} fusion(bf16[1,768,2048]{2,1,0:T(8,128)(2,1)} %get-tuple-element.157, f32[256]{0:T(256)S(1)} %get-tuple-element.300, f32[256,1536]{1,0:T(8,128)S(1)} %fusion.81), kind=kOutput, calls=%fused_computation.84 | convolution fusion | flops 807010304 | bytes 6816768 | tf_op jit(solution)/shard_map/cond/branch_1_fun/dot_general | solution.py:32
  149.8 3.9 %fusion.76 = bf16[256,2048]{1,0:T(8,128)(2,1)} fusion(bf16[1,768,2048]{2,1,0:T(8,128)(2,1)} %get-tuple-element.157, f32[256]{0:T(256)S(1)} %get-tuple-element.299, f32[256,1536]{1,0:T(8,128)S(1)} %fusion.79), kind=kOutput, calls=%fused_computation.85 | convolution fusion | flops 807534592 | bytes 5768192 | tf_op jit(solution)/shard_map/cond/branch_1_fun/dot_general | solution.py:32
  154.2 1.4 collective-permute-done.11
  156.1 2.4 collective-permute-done.19
  158.5 1.3 add_convert_fusion
  160.0 48.5 %conditional.10 = (bf16[1,256,2,768]{3,2,1,0:T(2,128)(2,1)}, bf16[1,192,2048]{2,1,0:T(8,128)(2,1)}, bf16[1,256,2,768]{3,2,1,0:T(2,128)(2,1)}, f32[256,2048]{1,0:T(8,128)}, bf16[256,2048]{1,0:T(8,128)(2,1)S(1)}) conditional(s32[]{:T(128)} %bitcast.4, (bf16[1,2048,2,768]{3,2,1,0:T(2,128)(2,1)}, bf16[1,768,2048]{2,1,0:T(8,128)(2,1)}, ...), branch_computations={%region_16.17_spmd, %region_17.18_spmd} | conditional | flops 6 | bytes 12583148 | solution.py:131
  160.0 2.6 %constant_dynamic-slice_fusion.5 = bf16[1,256,2,768]{3,2,1,0:T(2,128)(2,1)} fusion(bf16[1,2048,2,768]{3,2,1,0:T(2,128)(2,1)} %get-tuple-element.249, s32[]{:T(128)S(6)} %select_n.131), kind=kLoop, calls=%fused_computation.109 | loop fusion | bytes 1572868 | tf_op jit(solution)/shard_map/dynamic_slice | solution.py:88
  162.6 1.4 collective-permute-start.1
  164.0 1.3 constant_dynamic-slice_fusion.4
  165.4 1.0 collective-permute-start.2
  166.4 1.2 collective-permute-start.3
  167.6 22.5 %collective-permute-done.1 = bf16[1,256,2,768]{3,2,1,0:T(2,128)(2,1)} collective-permute-done((bf16[1,256,2,768]{3,2,1,0:T(2,128)(2,1)}, bf16[1,256,2,768]{3,2,1,0:T(2,128)(2,1)}, u32[]{:S(2)}, u32[]{:S(2)}) %collective-permute-start.1) | collective-permute-done | bytes 786464 | tf_op jit(solution)/shard_map/cond/branch_1_fun/ppermute | solution.py:18
  190.1 18.4 %collective-permute-done.2 = bf16[1,192,2048]{2,1,0:T(8,128)(2,1)} collective-permute-done((bf16[1,192,2048]{2,1,0:T(8,128)(2,1)S(1)}, bf16[1,192,2048]{2,1,0:T(8,128)(2,1)}, u32[]{:S(2)}, u32[]{:S(2)}) %collective-permute-start.2) | collective-permute-done | bytes 786464 | tf_op jit(solution)/shard_map/cond/branch_1_fun/ppermute | solution.py:18
  208.5 3.8 %fusion.98 = (bf16[256,2048]{1,0:T(8,128)(2,1)S(1)}, f32[256,2048]{1,0:T(8,128)}) fusion(bf16[256,2048]{1,0:T(8,128)(2,1)} %collective-permute-done.20, f32[256,2048]{1,0:T(8,128)} %get-tuple-element.291, bf16[256,2048]{1,0:T(8,128)(2,1)S(1)} %get-tuple-element.292), kind=kLoop, calls=%fused_computation.144 | loop fusion | flops 2621440 | bytes 7340032 | tf_op jit(solution)/shard_map/convert.3
  213.2 3.0 %collective-permute-start.21 = (bf16[64,2048]{1,0:T(8,128)(2,1)}, bf16[64,2048]{1,0:T(8,128)(2,1)S(1)}, u32[]{:S(2)}, u32[]{:S(2)}) collective-permute-start(bf16[64,2048]{1,0:T(8,128)(2,1)} %get-tuple-element.321), channel_id=1, source_target_pairs={{0,12},{1,13},{2,14},{3,15},{4,0},{5,1},{6,2},{7,3},{8,4},{9,5},{1... | collective-permute-start | bytes 786440 | tf_op jit(solution)/shard_map/ppermute | solution.py:206
  216.2 2.3 collective-permute-start.23
  218.5 31.9 %conditional.11 = ((bf16[1,2048,2,768]{3,2,1,0:T(2,128)(2,1)}, bf16[1,768,2048]{2,1,0:T(8,128)(2,1)})) conditional(s32[]{:T(128)} %bitcast.4, (bf16[1,2048,2,768]{3,2,1,0:T(2,128)(2,1)}, bf16[1,768,2048]{2,1,0:T(8,128)(2,1)}) %tuple.63, (s32[]{:T(128)}, bf16[1,256,2,768]{3,2,1,0:T(2,128)(2,1)}, bf16[1,256,2,768]{3,2,1,0:T(2,128)(2,1)S(1)}, ...), branch_computations={%region_18.19_spmd, %region_19.20_spmd} | conditional | flops 61 | bytes 34603864 | solution.py:159
  218.5 1.2 collective-permute-start.4
  220.0 4.2 %broadcast.113 = bf16[1,2048,2,768]{3,2,1,0:T(2,128)(2,1)} broadcast(bf16[]{:T(256)} %constant.157.clone), dimensions={} | broadcast | bytes 6291458 | tf_op jit(solution)/shard_map/broadcast.15
  224.1 2.6 %constant_dynamic-update-slice_fusion.11 = bf16[1,2048,2,768]{3,2,1,0:T(2,128)(2,1)} fusion(bf16[1,2048,2,768]{3,2,1,0:T(2,128)(2,1)} %broadcast.113, bf16[1,256,2,768]{3,2,1,0:T(2,128)(2,1)} %get-tuple-element.164, s32[]{:T(128)S(6)} %select_n.98), kind=kLoop, calls=%fused_computation.121 | loop fusion | bytes 1572868 | tf_op jit(solution)/shard_map/cond/branch_1_fun/dynamic_update_slice | solution.py:98
  226.7 1.4 constant_dynamic-update-slice_fusion.10
  228.1 1.4 constant_dynamic-update-slice_fusion.9
  229.5 2.6 %constant_dynamic-update-slice_fusion.8 = bf16[1,2048,2,768]{3,2,1,0:T(2,128)(2,1)} fusion(bf16[1,2048,2,768]{3,2,1,0:T(2,128)(2,1)} %constant_dynamic-update-slice_fusion.9, bf16[1,256,2,768]{3,2,1,0:T(2,128)(2,1)} %get-tuple-element.168, s32[]{:T(128)S(6)} %select_n.101), kind=kLoop, calls=%fused_computation.118 | loop fusion | bytes 1572868 | tf_op jit(solution)/shard_map/cond/branch_1_fun/dynamic_update_slice | solution.py:98
  232.1 2.1 broadcast.114
  235.1 2.6 %constant_dynamic-update-slice_fusion.7 = bf16[1,2048,2,768]{3,2,1,0:T(2,128)(2,1)} fusion(bf16[1,2048,2,768]{3,2,1,0:T(2,128)(2,1)} %constant_dynamic-update-slice_fusion.8, bf16[1,256,2,768]{3,2,1,0:T(2,128)(2,1)} %get-tuple-element.169, s32[]{:T(128)S(6)} %select_n.102), kind=kLoop, calls=%fused_computation.117 | loop fusion | bytes 1572868 | tf_op jit(solution)/shard_map/cond/branch_1_fun/dynamic_update_slice | solution.py:98
  237.6 2.6 %constant_dynamic-update-slice_fusion.6 = bf16[1,2048,2,768]{3,2,1,0:T(2,128)(2,1)} fusion(bf16[1,2048,2,768]{3,2,1,0:T(2,128)(2,1)} %constant_dynamic-update-slice_fusion.7, bf16[1,256,2,768]{3,2,1,0:T(2,128)(2,1)} %get-tuple-element.170, s32[]{:T(128)S(6)} %select_n.103), kind=kLoop, calls=%fused_computation.116 | loop fusion | bytes 1572868 | tf_op jit(solution)/shard_map/cond/branch_1_fun/dynamic_update_slice | solution.py:98
  240.2 2.6 %constant_dynamic-update-slice_fusion.5 = bf16[1,2048,2,768]{3,2,1,0:T(2,128)(2,1)} fusion(bf16[1,2048,2,768]{3,2,1,0:T(2,128)(2,1)} %constant_dynamic-update-slice_fusion.6, bf16[1,256,2,768]{3,2,1,0:T(2,128)(2,1)} %get-tuple-element.171, s32[]{:T(128)S(6)} %select_n.104), kind=kLoop, calls=%fused_computation.115 | loop fusion | bytes 1572868 | tf_op jit(solution)/shard_map/cond/branch_1_fun/dynamic_update_slice | solution.py:98
  242.7 2.1 constant_dynamic-update-slice_fusion.2
  244.8 2.1 constant_dynamic-update-slice_fusion.1
  246.9 2.6 %constant_dynamic-update-slice_fusion.4 = bf16[1,2048,2,768]{3,2,1,0:T(2,128)(2,1)} fusion(bf16[1,2048,2,768]{3,2,1,0:T(2,128)(2,1)} %constant_dynamic-update-slice_fusion.5, bf16[1,256,2,768]{3,2,1,0:T(2,128)(2,1)} %collective-permute-done.4, s32[]{:T(128)S(6)} %select_n.105), kind=kLoop, calls=%fused_computation.114 | loop fusion | bytes 1572868 | tf_op jit(solution)/shard_map/cond/branch_1_fun/dynamic_update_slice | solution.py:98
  250.4 1.3 fusion.95
  (70 shorter events, 10.2 us)
Async XLA Ops:
  0.6 6.9 %copy-start.4 = (bf16[1,768,2048]{2,1,0:T(8,128)(2,1)S(1)}, bf16[1,768,2048]{2,1,0:T(8,128)(2,1)}, u32[]{:S(2)}) copy-start(bf16[1,768,2048]{2,1,0:T(8,128)(2,1)} %param.29) | copy-start | bytes 9437188
  7.5 1.7 copy-start.8
  7.5 1.7 copy-start.9
  7.6 1.9 copy-start.10
  7.6 1.9 copy-start.11
  7.6 2.0 copy-start.12
  7.6 2.3 copy-start.6
  7.6 2.3 copy-start.7
  9.3 55.5 %copy-start.13 = (s32[8]{0:T(128)S(1)}, s32[8]{0:T(128)}, u32[]{:S(2)}) copy-start(s32[8]{0:T(128)} %param.27) | copy-start | bytes 100
  10.1 7.6 %collective-permute-start.12 = (bf16[64,2176]{1,0:T(8,128)(2,1)S(1)}, bf16[64,2176]{1,0:T(8,128)(2,1)S(1)}, u32[]{:S(2)}, u32[]{:S(2)}) collective-permute-start(bf16[64,2176]{1,0:T(8,128)(2,1)S(1)} %concatenate.22), channel_id=1, source_target_pairs={{0,4},{1,5},{2,6},{3,7},{4,8},{5,9},{6,10},{7,11},{8,12},{9,13},{1... | collective-permute-start | bytes 835592 | tf_op jit(solution)/shard_map/ppermute | solution.py:184
  11.5 23.2 %collective-permute-start.13 = (bf16[64,2176]{1,0:T(8,128)(2,1)S(1)}, bf16[64,2176]{1,0:T(8,128)(2,1)S(1)}, u32[]{:S(2)}, u32[]{:S(2)}) collective-permute-start(bf16[64,2176]{1,0:T(8,128)(2,1)S(1)} %concatenate.22), channel_id=1, source_target_pairs={{0,8},{1,9},{2,10},{3,11},{4,12},{5,13},{6,14},{7,15},{8,0},{9,1},... | collective-permute-start | bytes 835592 | tf_op jit(solution)/shard_map/ppermute | solution.py:184
  12.6 25.0 %collective-permute-start.14 = (bf16[64,2176]{1,0:T(8,128)(2,1)S(1)}, bf16[64,2176]{1,0:T(8,128)(2,1)S(1)}, u32[]{:S(2)}, u32[]{:S(2)}) collective-permute-start(bf16[64,2176]{1,0:T(8,128)(2,1)S(1)} %concatenate.22), channel_id=1, source_target_pairs={{0,12},{1,13},{2,14},{3,15},{4,0},{5,1},{6,2},{7,3},{8,4},{9,5},{1... | collective-permute-start | bytes 835592 | tf_op jit(solution)/shard_map/ppermute | solution.py:184
  37.6 25.8 %collective-permute-start.15 = (bf16[256,2176]{1,0:T(8,128)(2,1)S(1)}, bf16[256,2176]{1,0:T(8,128)(2,1)}, u32[]{:S(2)}, u32[]{:S(2)}) collective-permute-start(bf16[256,2176]{1,0:T(8,128)(2,1)S(1)} %pad_maximum_fusion), channel_id=1, source_target_pairs={{0,2},{1,3},{2,0},{3,1},{4,6},{5,7},{6,4},{7,5},{8,10},{9,11},{10,... | collective-permute-start | bytes 3342344 | tf_op jit(solution)/shard_map/ppermute | solution.py:18
  37.9 57.8 %collective-permute-start.17 = (bf16[256,2176]{1,0:T(8,128)(2,1)S(1)}, bf16[256,2176]{1,0:T(8,128)(2,1)}, u32[]{:S(2)}, u32[]{:S(2)}) collective-permute-start(bf16[256,2176]{1,0:T(8,128)(2,1)S(1)} %pad_maximum_fusion), channel_id=1, source_target_pairs={{0,1},{1,0},{2,3},{3,2},{4,5},{5,4},{6,7},{7,6},{8,9},{9,8},{10,11... | collective-permute-start | bytes 3342344 | tf_op jit(solution)/shard_map/ppermute | solution.py:18
  63.4 68.5 %collective-permute-start.16 = (bf16[256,2176]{1,0:T(8,128)(2,1)}, bf16[256,2176]{1,0:T(8,128)(2,1)}, u32[]{:S(2)}, u32[]{:S(2)}) collective-permute-start(bf16[256,2176]{1,0:T(8,128)(2,1)} %collective-permute-done.15), channel_id=1, source_target_pairs={{0,1},{1,0},{2,3},{3,2},{4,5},{5,4},{6,7},{7,6},{8,9},{9,8},{10,11... | collective-permute-start | bytes 3342344 | tf_op jit(solution)/shard_map/ppermute | solution.py:18
  67.7 17.6 %collective-permute-start = (bf16[1,256,2,768]{3,2,1,0:T(2,128)(2,1)S(1)}, bf16[1,256,2,768]{3,2,1,0:T(2,128)(2,1)}, u32[]{:S(2)}, u32[]{:S(2)}) collective-permute-start(bf16[1,256,2,768]{3,2,1,0:T(2,128)(2,1)S(1)} %constant_dynamic-slice_fusion.1), channel_id=1, source_target_pairs={{0,8},{1,9},{2,10},{3,11},{4,12},{5,13},{6,14},{7,15},{8,0},{9,1},... | collective-permute-start | bytes 2359304 | tf_op jit(solution)/shard_map/cond/branch_1_fun/ppermute | solution.py:18
  96.0 26.4 %collective-permute-start.6 = (bf16[1,256,2,768]{3,2,1,0:T(2,128)(2,1)S(1)}, bf16[1,256,2,768]{3,2,1,0:T(2,128)(2,1)}, u32[]{:S(2)}, u32[]{:S(2)}) collective-permute-start(bf16[1,256,2,768]{3,2,1,0:T(2,128)(2,1)S(1)} %get-tuple-element.138), channel_id=1, source_target_pairs={{0,8},{1,9},{2,10},{3,11},{4,12},{5,13},{6,14},{7,15},{8,0},{9,1},... | collective-permute-start | bytes 2359304 | tf_op jit(solution)/shard_map/cond/branch_1_fun/ppermute | solution.py:18
  98.9 31.9 %collective-permute-start.7 = (bf16[1,192,2048]{2,1,0:T(8,128)(2,1)S(1)}, bf16[1,192,2048]{2,1,0:T(8,128)(2,1)}, u32[]{:S(2)}, u32[]{:S(2)}) collective-permute-start(bf16[1,192,2048]{2,1,0:T(8,128)(2,1)S(1)} %get-tuple-element.139), channel_id=1, source_target_pairs={{0,8},{1,9},{2,10},{3,11},{4,12},{5,13},{6,14},{7,15},{8,0},{9,1},... | collective-permute-start | bytes 2359304 | tf_op jit(solution)/shard_map/cond/branch_1_fun/ppermute | solution.py:18
  99.0 32.9 %collective-permute-start.8 = (bf16[1,256,2,768]{3,2,1,0:T(2,128)(2,1)}, bf16[1,256,2,768]{3,2,1,0:T(2,128)(2,1)}, u32[]{:S(2)}, u32[]{:S(2)}) collective-permute-start(bf16[1,256,2,768]{3,2,1,0:T(2,128)(2,1)} %get-tuple-element.140), channel_id=1, source_target_pairs={{0,16},{16,0},{1,17},{17,1},{2,18},{18,2},{3,19},{19,3},{4,20},{20... | collective-permute-start | bytes 2359304 | tf_op jit(solution)/shard_map/cond/branch_1_fun/ppermute | solution.py:124
  100.3 4.7 %copy-start.1 = (bf16[2048,1536]{1,0:T(8,128)(2,1)S(1)}, bf16[2048,1536]{1,0:T(8,128)(2,1)}, u32[]{:S(2)}) copy-start(bf16[2048,1536]{1,0:T(8,128)(2,1)} %get-tuple-element.142) | copy-start | bytes 18874372 | tf_op jit(solution)/shard_map/conditional
  131.9 1.4 copy-start.5
  133.3 20.3 %collective-permute-start.9 = (bf16[1,256,2,768]{3,2,1,0:T(2,128)(2,1)S(1)}, bf16[1,256,2,768]{3,2,1,0:T(2,128)(2,1)S(1)}, u32[]{:S(2)}, u32[]{:S(2)}) collective-permute-start(bf16[1,256,2,768]{3,2,1,0:T(2,128)(2,1)S(1)} %get-tuple-element.152), channel_id=1, source_target_pairs={{0,8},{1,9},{2,10},{3,11},{4,12},{5,13},{6,14},{7,15},{8,0},{9,1},... | collective-permute-start | bytes 2359304 | tf_op jit(solution)/shard_map/cond/branch_1_fun/ppermute | solution.py:18
  136.3 18.0 %collective-permute-start.10 = (bf16[1,256,2,768]{3,2,1,0:T(2,128)(2,1)S(1)}, bf16[1,256,2,768]{3,2,1,0:T(2,128)(2,1)}, u32[]{:S(2)}, u32[]{:S(2)}) collective-permute-start(bf16[1,256,2,768]{3,2,1,0:T(2,128)(2,1)S(1)} %get-tuple-element.153), channel_id=1, source_target_pairs={{0,16},{16,0},{1,17},{17,1},{2,18},{18,2},{3,19},{19,3},{4,20},{20... | collective-permute-start | bytes 2359304 | tf_op jit(solution)/shard_map/cond/branch_1_fun/ppermute | solution.py:124
  137.5 18.1 %collective-permute-start.11 = (bf16[1,192,2048]{2,1,0:T(8,128)(2,1)S(1)}, bf16[1,192,2048]{2,1,0:T(8,128)(2,1)}, u32[]{:S(2)}, u32[]{:S(2)}) collective-permute-start(bf16[1,192,2048]{2,1,0:T(8,128)(2,1)S(1)} %get-tuple-element.154), channel_id=1, source_target_pairs={{0,16},{16,0},{1,17},{17,1},{2,18},{18,2},{3,19},{19,3},{4,20},{20... | collective-permute-start | bytes 2359304 | tf_op jit(solution)/shard_map/cond/branch_1_fun/ppermute | solution.py:124
  137.7 5.0 %copy-start.3 = (bf16[2048,1536]{1,0:T(8,128)(2,1)S(1)}, bf16[2048,1536]{1,0:T(8,128)(2,1)}, u32[]{:S(2)}) copy-start(bf16[2048,1536]{1,0:T(8,128)(2,1)} %get-tuple-element.156) | copy-start | bytes 18874372 | tf_op jit(solution)/shard_map/conditional.1
  155.6 2.9 %collective-permute-start.19 = (bf16[256,2048]{1,0:T(8,128)(2,1)}, bf16[256,2048]{1,0:T(8,128)(2,1)S(1)}, u32[]{:S(2)}, u32[]{:S(2)}) collective-permute-start(bf16[256,2048]{1,0:T(8,128)(2,1)} %get-tuple-element.208), channel_id=1, source_target_pairs={{0,1},{1,0},{2,3},{3,2},{4,5},{5,4},{6,7},{7,6},{8,9},{9,8},{10,11... | collective-permute-start | bytes 3145736 | tf_op jit(solution)/shard_map/ppermute | solution.py:18
  155.6 4.4 %collective-permute-start.18 = (bf16[256,2048]{1,0:T(8,128)(2,1)}, bf16[256,2048]{1,0:T(8,128)(2,1)S(1)}, u32[]{:S(2)}, u32[]{:S(2)}) collective-permute-start(bf16[256,2048]{1,0:T(8,128)(2,1)} %get-tuple-element.204), channel_id=1, source_target_pairs={{0,1},{1,0},{2,3},{3,2},{4,5},{5,4},{6,7},{7,6},{8,9},{9,8},{10,11... | collective-permute-start | bytes 3145736 | tf_op jit(solution)/shard_map/ppermute | solution.py:18
  159.8 48.7 %collective-permute-start.20 = (bf16[256,2048]{1,0:T(8,128)(2,1)}, bf16[256,2048]{1,0:T(8,128)(2,1)}, u32[]{:S(2)}, u32[]{:S(2)}) collective-permute-start(bf16[256,2048]{1,0:T(8,128)(2,1)} %add_convert_fusion), channel_id=1, source_target_pairs={{0,2},{1,3},{2,0},{3,1},{4,6},{5,7},{6,4},{7,5},{8,10},{9,11},{10,... | collective-permute-start | bytes 3145736 | tf_op jit(solution)/shard_map/ppermute | solution.py:18
  162.6 27.5 %collective-permute-start.1 = (bf16[1,256,2,768]{3,2,1,0:T(2,128)(2,1)}, bf16[1,256,2,768]{3,2,1,0:T(2,128)(2,1)}, u32[]{:S(2)}, u32[]{:S(2)}) collective-permute-start(bf16[1,256,2,768]{3,2,1,0:T(2,128)(2,1)} %constant_dynamic-slice_fusion.5), channel_id=1, source_target_pairs={{0,8},{1,9},{2,10},{3,11},{4,12},{5,13},{6,14},{7,15},{8,0},{9,1},... | collective-permute-start | bytes 2359304 | tf_op jit(solution)/shard_map/cond/branch_1_fun/ppermute | solution.py:18
  165.4 43.1 %collective-permute-start.2 = (bf16[1,192,2048]{2,1,0:T(8,128)(2,1)S(1)}, bf16[1,192,2048]{2,1,0:T(8,128)(2,1)}, u32[]{:S(2)}, u32[]{:S(2)}) collective-permute-start(bf16[1,192,2048]{2,1,0:T(8,128)(2,1)S(1)} %constant_dynamic-slice_fusion.4), channel_id=1, source_target_pairs={{0,8},{1,9},{2,10},{3,11},{4,12},{5,13},{6,14},{7,15},{8,0},{9,1},... | collective-permute-start | bytes 2359304 | tf_op jit(solution)/shard_map/cond/branch_1_fun/ppermute | solution.py:18
  166.4 42.1 %collective-permute-start.3 = (bf16[1,256,2,768]{3,2,1,0:T(2,128)(2,1)S(1)}, bf16[1,256,2,768]{3,2,1,0:T(2,128)(2,1)}, u32[]{:S(2)}, u32[]{:S(2)}) collective-permute-start(bf16[1,256,2,768]{3,2,1,0:T(2,128)(2,1)S(1)} %get-tuple-element.161), channel_id=1, source_target_pairs={{0,16},{16,0},{1,17},{17,1},{2,18},{18,2},{3,19},{19,3},{4,20},{20... | collective-permute-start | bytes 2359304 | tf_op jit(solution)/shard_map/cond/branch_1_fun/ppermute | solution.py:124
  213.2 37.2 %collective-permute-start.21 = (bf16[64,2048]{1,0:T(8,128)(2,1)}, bf16[64,2048]{1,0:T(8,128)(2,1)S(1)}, u32[]{:S(2)}, u32[]{:S(2)}) collective-permute-start(bf16[64,2048]{1,0:T(8,128)(2,1)} %get-tuple-element.321), channel_id=1, source_target_pairs={{0,12},{1,13},{2,14},{3,15},{4,0},{5,1},{6,2},{7,3},{8,4},{9,5},{1... | collective-permute-start | bytes 786440 | tf_op jit(solution)/shard_map/ppermute | solution.py:206
  216.2 34.2 %collective-permute-start.22 = (bf16[64,2048]{1,0:T(8,128)(2,1)}, bf16[64,2048]{1,0:T(8,128)(2,1)}, u32[]{:S(2)}, u32[]{:S(2)}) collective-permute-start(bf16[64,2048]{1,0:T(8,128)(2,1)} %get-tuple-element.323), channel_id=1, source_target_pairs={{0,8},{1,9},{2,10},{3,11},{4,12},{5,13},{6,14},{7,15},{8,0},{9,1},... | collective-permute-start | bytes 786440 | tf_op jit(solution)/shard_map/ppermute | solution.py:206
  216.2 34.2 %collective-permute-start.23 = (bf16[64,2048]{1,0:T(8,128)(2,1)}, bf16[64,2048]{1,0:T(8,128)(2,1)}, u32[]{:S(2)}, u32[]{:S(2)}) collective-permute-start(bf16[64,2048]{1,0:T(8,128)(2,1)} %get-tuple-element.322), channel_id=1, source_target_pairs={{0,4},{1,5},{2,6},{3,7},{4,8},{5,9},{6,10},{7,11},{8,12},{9,13},{1... | collective-permute-start | bytes 786440 | tf_op jit(solution)/shard_map/ppermute | solution.py:206
  218.5 28.4 %collective-permute-start.4 = (bf16[1,256,2,768]{3,2,1,0:T(2,128)(2,1)}, bf16[1,256,2,768]{3,2,1,0:T(2,128)(2,1)}, u32[]{:S(2)}, u32[]{:S(2)}) collective-permute-start(bf16[1,256,2,768]{3,2,1,0:T(2,128)(2,1)} %get-tuple-element.168), channel_id=1, source_target_pairs={{0,16},{16,0},{1,17},{17,1},{2,18},{18,2},{3,19},{19,3},{4,20},{20... | collective-permute-start | bytes 2359304 | tf_op jit(solution)/shard_map/cond/branch_1_fun/ppermute | solution.py:143
  219.7 29.7 %collective-permute-start.5 = (bf16[1,192,2048]{2,1,0:T(8,128)(2,1)}, bf16[1,192,2048]{2,1,0:T(8,128)(2,1)S(1)}, u32[]{:S(2)}, u32[]{:S(2)}) collective-permute-start(bf16[1,192,2048]{2,1,0:T(8,128)(2,1)} %get-tuple-element.173), channel_id=1, source_target_pairs={{0,16},{16,0},{1,17},{17,1},{2,18},{18,2},{3,19},{19,3},{4,20},{20... | collective-permute-start | bytes 2359304 | tf_op jit(solution)/shard_map/cond/branch_1_fun/ppermute | solution.py:143

commit v2 on v1

--- a/solution.py
+++ b/solution.py
@@ -1,6 +1,11 @@
+import functools
+import math
+
 import jax
 import jax.numpy as jnp
 from jax import lax
+from jax.experimental import pallas as pl
+from jax.experimental.pallas import tpu as pltpu
 from jax.sharding import PartitionSpec as P
 
 LANES = 128
@@ -83,82 +88,60 @@
     return weight * expert_ffn(piece[:, :width], joined_w, down_w)
 
 
-def half_piece(array, axis, half, index, count):
-    rows = array.shape[axis] // (2 * count)
-    return lax.dynamic_slice_in_dim(array, (half * count + index) * rows, rows, axis=axis)
-
-
-def assemble(shape, axis, group, own_parts, other_parts):
-    result = jnp.zeros(shape, jnp.bfloat16)
-    count = len(own_parts)
-    rows = shape[axis] // (2 * count)
-    for parts, half in ((own_parts, group), (other_parts, 1 - group)):
-        for index, part in enumerate(parts):
-            start = (half * count + index) * rows
-            result = lax.dynamic_update_slice_in_dim(result, part, start, axis=axis)
-    return result
-
-
-def swap_steps(on, group, gate_up, down, plan):
-    half_bit = lax.axis_size("expert") // 2
-    counts = (
-        sum(1 for step in plan for name, _ in step if name == "g"),
-        sum(1 for step in plan for name, _ in step if name == "d"),
-    )
-    arrived, relayed, pending = {}, {}, []
-
-    def cut(item):
-        name, index = item
-        if name == "g":
-            return half_piece(gate_up, 1, group, index, counts[0])
-        return half_piece(down, 1, group, index, counts[1])
-
-    def step(items, work):
-        nonlocal pending
-        outgoing = [cut(item) for item in items]
-        to_relay = [arrived[item] for item in pending]
-
-        def active(args):
-            outgoing, to_relay = args
-            crossed = [exchange(value, half_bit) for value in outgoing]
-            handed = [lax.ppermute(value, "groups", [(0, 1), (1, 0)]) for value in to_relay]
-            return crossed, handed, work()
-
-        def idle(args):
-            outgoing, to_relay = args
-            return list(outgoing), list(to_relay), work()
-
-        crossed, handed, made = lax.cond(on, active, idle, (outgoing, to_relay))
-        for item, value in zip(pending, handed):
-            relayed[item] = value
-        for item, value in zip(items, crossed):
-            arrived[item] = value
-        pending = list(items)
-        return made
-
-    def finish():
-        to_relay = [arrived[item] for item in pending]
-
-        def active(to_relay):
-            handed = [lax.ppermute(value, "groups", [(0, 1), (1, 0)]) for value in to_relay]
-            for item, value in zip(pending, handed):
-                relayed[item] = value
-            whole = []
-            for name, count, like in (("g", counts[0], gate_up), ("d", counts[1], down)):
-                whole.append(
-                    assemble(
-                        like.shape,
-                        1,
-                        group,
-                        [arrived[name, index] for index in range(count)],
-                        [relayed[name, index] for index in range(count)],
-                    )
-                )
-            return tuple(whole)
-
-        return lax.cond(on, active, lambda _: (gate_up, down), to_relay)
-
-    return step, finish
+def half_piece(array, half, index, count):
+    rows = array.shape[1] // (2 * count)
+    return lax.dynamic_slice_in_dim(array, (half * count + index) * rows, rows, axis=1)
+
+
+def copies_kernel(places, group_ref, *refs):
+    count = len(places)
+    sources, outputs = refs[:count], refs[-4 - count : -2 - count]
+    held, in_sems, out_sems = refs[-2 - count : -2], refs[-2], refs[-1]
+    group = group_ref[0]
+    inward, outward = [], []
+    for number, (source, place) in enumerate(zip(sources, places)):
+        if len(place) == 5:
+            output, mine, first, span, rows = place
+            half = group if mine else 1 - group
+            start = pl.multiple_of(half * span + first, 16)
+        else:
+            output, start, rows = place
+            source = source.at[:, pl.ds(start, rows)]
+        target = outputs[output].at[:, pl.ds(start, rows)]
+        inward.append(pltpu.make_async_copy(source, held[number], in_sems.at[number]))
+        outward.append(pltpu.make_async_copy(held[number], target, out_sems.at[number]))
+    for copy in inward:
+        copy.start()
+    for arrival, departure in zip(inward, outward):
+        arrival.wait()
+        departure.start()
+    for departure in outward:
+        departure.wait()
+
+
+def place_pieces(group, sources, places, likes, onto=None):
+    count = len(sources)
+    anywhere = pl.BlockSpec(memory_space=pl.ANY)
+    extra = list(onto) if onto is not None else []
+    held = [
+        pltpu.VMEM((source.shape[0], place[-1], *source.shape[2:]), source.dtype)
+        for source, place in zip(sources, places)
+    ]
+    moved = sum(math.prod(one.shape) * one.dtype.itemsize for one in held)
+    return pl.pallas_call(
+        functools.partial(copies_kernel, places),
+        out_shape=[jax.ShapeDtypeStruct(like.shape, like.dtype) for like in likes],
+        in_specs=[pl.BlockSpec(memory_space=pltpu.SMEM)] + [anywhere] * (count + len(extra)),
+        out_specs=[anywhere] * len(likes),
+        scratch_shapes=[
+            *held,
+            pltpu.SemaphoreType.DMA((count,)),
+            pltpu.SemaphoreType.DMA((count,)),
+        ],
+        input_output_aliases={1 + count + k: k for k in range(len(extra))},
+        cost_estimate=pl.CostEstimate(flops=0, bytes_accessed=2 * moved, transcendentals=0),
+        compiler_params=pltpu.CompilerParams(vmem_limit_bytes=moved + (4 << 20)),
+    )(group.reshape(1), *sources, *extra)
 
 
 PLAN = (
@@ -167,39 +150,107 @@
     (("g", 2),),
     (("g", 3), ("d", 1)),
 )
-
-
-def staged(
-    tokens, chosen, gates, placement, gate_up, down, step, finish
-):
+COUNTS = {
+    name: sum(1 for items in PLAN for kind, _ in items if kind == name) for name in ("g", "d")
+}
+GROUP_PAIRS = [(0, 1), (1, 0)]
+
+
+class Swap:
+    def __init__(self, on, group, gate_up, down):
+        self.on, self.group = on, group
+        self.source = {"g": gate_up, "d": down}
+        self.half_bit = lax.axis_size("expert") // 2
+        self.arrived, self.relayed, self.pending = {}, {}, ()
+        self.ready = self.cut(PLAN[0])
+
+    def cut(self, items):
+        return [half_piece(self.source[n], self.group, k, COUNTS[n]) for n, k in items]
+
+    def step(self, turn, work):
+        items = PLAN[turn]
+        outgoing = self.ready
+        to_relay = [self.arrived[item] for item in self.pending]
+        following = PLAN[turn + 1] if turn + 1 < len(PLAN) else ()
+
+        def active(args):
+            outgoing, to_relay = args
+            crossed = [exchange(value, self.half_bit) for value in outgoing]
+            handed = [lax.ppermute(value, "groups", GROUP_PAIRS) for value in to_relay]
+            return crossed, handed, lax.optimization_barrier((self.cut(following), work()))
+
+        def idle(args):
+            outgoing, to_relay = args
+            return list(outgoing), list(to_relay), ([*self.cut(following)], work())
+
+        crossed, handed, (self.ready, made) = lax.cond(self.on, active, idle, (outgoing, to_relay))
+        self.relayed.update(zip(self.pending, handed))
+        self.arrived.update(zip(items, crossed))
+        self.pending = items
+        return made
+
+    def place(self, item, mine):
+        name, index = item
+        rows = self.source[name].shape[1]
+        size = rows // (2 * COUNTS[name])
+        return (0 if name == "g" else 1, mine, index * size, rows // 2, size)
+
+    def finish(self):
+        likes = (self.source["g"], self.source["d"])
+        last = self.pending
+        to_relay = [self.arrived[item] for item in last]
+
+        def active(to_relay):
+            handed = [lax.ppermute(value, "groups", GROUP_PAIRS) for value in to_relay]
+            sources = list(self.arrived.values()) + list(self.relayed.values())
+            places = [self.place(item, True) for item in self.arrived]
+            places += [self.place(item, False) for item in self.relayed]
+            partial_pair = place_pieces(self.group, sources, places, likes)
+            return tuple(
+                place_pieces(
+                    self.group, handed, [self.place(item, False) for item in last], likes, partial_pair
+                )
+            )
+
+        def idle(_):
+            places = []
+            for output, like in enumerate(likes):
+                rows = like.shape[1] // 4
+                places += [(output, index * rows, rows) for index in range(4)]
+            return tuple(place_pieces(self.group, [likes[p[0]] for p in places], places, likes))
+
+        return lax.cond(self.on, active, idle, to_relay)
+
+
+def staged(tokens, chosen, gates, placement, gate_up, down, swap):
     peers = lax.axis_size("expert")
     levels = peers // 4
     rows, width = tokens.shape
     own = extended_rows(tokens, chosen, gates, placement)
 
-    joined = lambda: gate_up[0].reshape(width, -1)
-    ffn = lambda piece, joined_w: weighted_ffn(piece, width, peers, joined_w, down[0])
+    def ffn(first, second, joined_w):
+        piece = jnp.concatenate([first, second], axis=0)
+        part = weighted_ffn(piece, width, peers, joined_w, down[0])
+        count = first.shape[0]
+        return part[:count], part[count:].astype(jnp.bfloat16)
 
     columns = [own] + [
         lax.ppermute(own, "expert", shift_pairs(peers, 4 * hop)) for hop in range(1, levels)
     ]
-    joined_w = step(PLAN[0], joined)
+    joined_w = swap.step(0, lambda: gate_up[0].reshape(width, -1))
+    columns, joined_w = lax.optimization_barrier((columns, joined_w))
     here = jnp.concatenate(columns, axis=0)
+    here_core = exchange(here, 1)
     across = exchange(here, 2)
-    here_core = exchange(here, 1)
-    part_here, part_here_core = step(
-        PLAN[1], lambda: (ffn(here, joined_w), ffn(here_core, joined_w).astype(jnp.bfloat16))
-    )
+    part_here, part_here_core = swap.step(1, lambda: ffn(here, here_core, joined_w))
+    across, part_here_core = lax.optimization_barrier((across, part_here_core))
     across_core = exchange(across, 1)
     got_here = exchange(part_here_core, 1)
-    part_across, part_across_core = step(
-        PLAN[2],
-        lambda: (ffn(across, joined_w), ffn(across_core, joined_w).astype(jnp.bfloat16)),
-    )
+    part_across, part_across_core = swap.step(2, lambda: ffn(across, across_core, joined_w))
     got_across = exchange(part_across_core, 1)
     sum_across = (part_across + got_across.astype(jnp.float32)).astype(jnp.bfloat16)
     got_column = exchange(sum_across, 2)
-    sum_here = step(PLAN[3], lambda: part_here + got_here.astype(jnp.float32))
+    sum_here = swap.step(3, lambda: part_here + got_here.astype(jnp.float32))
     column = sum_here + got_column.astype(jnp.float32)
     total = column[:rows]
     returned = [
@@ -210,7 +261,7 @@
         )
         for hop in range(1, levels)
     ]
-    new_gate_up, new_down = finish()
+    new_gate_up, new_down = swap.finish()
     for value in returned:
         total = total + value.astype(jnp.float32)
     total = total.astype(jnp.bfloat16)
@@ -234,7 +285,7 @@
     own_index = lax.axis_index("expert")
     group = lax.axis_index("groups")
     swap_here = swap_flags[own_index % half_count] == 1
-    step, finish = swap_steps(swap_here, group, gate_up, down, PLAN)
+    swap = Swap(swap_here, group, gate_up, down)
     if lax.axis_size("tensor") == 1 and peer_total == 16:
         count = tokens_one.shape[0]
         total, new_gate_up, new_down = staged(
@@ -244,8 +295,7 @@
             old_placement,
             gate_up,
             down,
-            step,
-            finish,
+            swap,
         )
         return (total[:count], total[count:], new_gate_up, new_down)
     slot_index = jnp.arange(peer_total, dtype=jnp.int32)
@@ -258,9 +308,9 @@
     ):
         rows = lax.all_gather(tokens, "tensor", axis=0, tiled=True)
         outs.append(routed_layer(rows, chosen, gates, old_slots, joined_w, down[0]))
-    for items in PLAN:
-        step(items, lambda: ())
-    new_gate_up, new_down = finish()
+    for turn in range(len(PLAN)):
+        swap.step(turn, lambda: ())
+    new_gate_up, new_down = swap.finish()
     return (outs[0], outs[1], new_gate_up, new_down)
 
 

time: 250 us -> 266 us (1.064)
  the two profiles are of different devices: /device:TPU:11 before, /device:TPU:8 now
where the time goes in v2:
time: 266 us; the launch traced here: 264 us
  waiting for transfers between devices  154 us (58%)
  local copies, waits for them, and re-layouts  40.8 us (15%)
  starting transfers between devices  31.1 us (12%)
  matrix products  15.1 us (6%)
  other arithmetic  14.2 us (5%)
  Pallas kernels  7.53 us (3%)
    ppermute x12, waiting for transfers between devices, exchange(): lax.ppermute(value, 'expert', xor_pairs(lax.axis_size('expert'), mask))  118 us
    ppermute x6, waiting for transfers between devices, active(): handed = [lax.ppermute(value, 'groups', GROUP_PAIRS) for value in to_relay]  35.8 us
    cond x15, local copies, waits for them, and re-layouts  17.1 us
    dynamic_slice x6, local copies, waits for them, and re-layouts, half_piece(): lax.dynamic_slice_in_dim(array, (half * count + index) * rows, rows, axis=1)  11.7 us
    dot_general x2, matrix products, expert_ffn(): projected = jnp.dot(rows, joined_w, preferred_element_type=jnp.float32)  11.4 us
    ppermute x12, starting transfers between devices, exchange(): lax.ppermute(value, 'expert', xor_pairs(lax.axis_size('expert'), mask))  11.3 us
    pallas_call x2, Pallas kernels, place_pieces(): pl.pallas_call(functools.partial(copies_kernel, places), out_shape=[jax.S...  7.53 us
    ppermute x3, starting transfers between devices, staged(): lax.ppermute(column[hop * rows:(hop + 1) * rows].astype(jnp.bfloat16), 'e...  7.2 us
  transfers between devices with their start and end apart: 24, of which 12 were waited for; matrix products, arithmetic and copies ran while one was open for 20% of the time, Pallas kernels for 3%

profile of v2, /device:TPU:8, one launch (start us, length us, event | category | flops | bytes accessed | tf_op | source)
XLA Modules:
  0.0 264.1 jit_solution(13398056518574748588)
XLA Ops:
  0.6 0.8 fusion.36
  1.4 0.8 broadcast_divide_fusion
  2.2 0.8 pad_add_fusion
  3.0 0.7 select_reduce_fusion.4
  4.1 1.0 pad_maximum_fusion
  5.2 3.0 %collective-permute-start.13 = (bf16[64,2176]{1,0:T(8,128)(2,1)S(1)}, bf16[64,2176]{1,0:T(8,128)(2,1)S(1)}, u32[]{:S(2)}, u32[]{:S(2)}) collective-permute-start(bf16[64,2176]{1,0:T(8,128)(2,1)S(1)} %concatenate.34), channel_id=1, source_target_pairs={{0,8},{1,9},{2,10},{3,11},{4,12},{5,13},{6,14},{7,15},{8,0},{9,1},... | collective-permute-start | bytes 835592 | tf_op jit(solution)/shard_map/ppermute | solution.py:238
  8.3 2.5 collective-permute-start.12
  10.8 2.6 constant_dynamic-slice_fusion.10
  14.5 43.6 %conditional.5 = (bf16[1,256,2,768]{3,2,1,0:T(2,128)(2,1)}, bf16[1,256,2,768]{3,2,1,0:T(2,128)(2,1)}, bf16[1,192,2048]{2,1,0:T(8,128)(2,1)}, bf16[2048,1536]{1,0:T(8,128)(2,1)}) conditional(s32[]{:T(128)} %bitcast.6, (s32[]{:T(128)}, bf16[1,2048,2,768]{3,2,1,0:T(2,128)(2,1)}, bf16[1,768,2048]{2,1,0:T(8,128)(2,1)}, ...), branch_computations={%region_2.3_spmd, %region_3.4_spmd} | conditional | flops 10 | bytes 20447428 | solution.py:186
  14.6 1.0 collective-permute-start.2
  15.5 6.8 %copy.22 = bf16[256,8,2,768]{3,1,2,0:T(8,128)(2,1)} copy(bf16[256,8,2,768]{3,2,1,0:T(2,128)(2,1)} %bitcast.26) | data formatting | bytes 12582912 | tf_op jit(solution)/shard_map/cond
  22.4 2.6 constant_dynamic-slice_fusion.3
  25.0 2.2 constant_dynamic-slice_fusion.2
  27.2 30.1 %collective-permute-done.2 = bf16[1,256,2,768]{3,2,1,0:T(2,128)(2,1)S(1)} collective-permute-done((bf16[1,256,2,768]{3,2,1,0:T(2,128)(2,1)}, bf16[1,256,2,768]{3,2,1,0:T(2,128)(2,1)S(1)}, u32[]{:S(2)}, u32[]{:S(2)}) %collective-permute-start.2) | collective-permute-done | bytes 786464 | tf_op jit(solution)/shard_map/cond/branch_1_fun/ppermute | solution.py:23
  57.2 0.9 copy.33
  58.1 0.7 constant_dynamic-update-slice_fusion.11
  58.9 0.7 constant_dynamic-update-slice_fusion.10
  59.6 0.7 constant_dynamic-update-slice_fusion.9
  60.4 0.7 constant_dynamic-update-slice_fusion.8
  61.1 3.0 %collective-permute-done.16 = bf16[256,2176]{1,0:T(8,128)(2,1)S(1)} collective-permute-done((bf16[256,2176]{1,0:T(8,128)(2,1)}, bf16[256,2176]{1,0:T(8,128)(2,1)S(1)}, u32[]{:S(2)}, u32[]{:S(2)}) %collective-permute-start.16) | collective-permute-done | bytes 1114144 | tf_op jit(solution)/shard_map/ppermute | solution.py:23
  64.0 53.7 %conditional.6 = (bf16[1,256,2,768]{3,2,1,0:T(2,128)(2,1)}, bf16[1,192,2048]{2,1,0:T(8,128)(2,1)}, bf16[1,256,2,768]{3,2,1,0:T(2,128)(2,1)}, bf16[1,256,2,768]{3...) conditional(s32[]{:T(128)} %bitcast.6, (s32[]{:T(128)}, ...), branch_computations={%region_4.6_spmd, %region_6.8_spmd} | conditional | flops 4835639808 | bytes 59644712 | solution.py:186
  64.1 3.3 %collective-permute-start.6 = (bf16[1,256,2,768]{3,2,1,0:T(2,128)(2,1)}, bf16[1,256,2,768]{3,2,1,0:T(2,128)(2,1)}, u32[]{:S(2)}, u32[]{:S(2)}) collective-permute-start(bf16[1,256,2,768]{3,2,1,0:T(2,128)(2,1)} %get-tuple-element.156), channel_id=1, source_target_pairs={{0,8},{1,9},{2,10},{3,11},{4,12},{5,13},{6,14},{7,15},{8,0},{9,1},... | collective-permute-start | bytes 2359304 | tf_op jit(solution)/shard_map/cond/branch_1_fun/ppermute | solution.py:23
  67.4 1.5 collective-permute-start.8
  68.9 1.3 constant_dynamic-update-slice_fusion.3
  70.4 5.7 %fusion.9 = f32[512,1536]{1,0:T(8,128)S(1)} fusion(bf16[2048,1536]{1,0:T(8,128)(2,1)} %get-tuple-element.163, bf16[512,2176]{1,0:T(8,128)(2,1)S(1)} %constant_dynamic-update-slice_fusion.2), kind=kOutput, calls=%fused_computation.26 | convolution fusion | flops 3221225472 | bytes 11534336 | tf_op jit(solution)/shard_map/cond/branch_1_fun/dot_general | solution.py:33
  76.2 1.9 convolution_multiply_fusion.1
  78.2 1.5 slice.113
  79.8 2.6 constant_dynamic-slice_fusion.5
  82.3 16.5 %collective-permute-done.6 = bf16[1,256,2,768]{3,2,1,0:T(2,128)(2,1)} collective-permute-done((bf16[1,256,2,768]{3,2,1,0:T(2,128)(2,1)}, bf16[1,256,2,768]{3,2,1,0:T(2,128)(2,1)}, u32[]{:S(2)}, u32[]{:S(2)}) %collective-permute-start.6) | collective-permute-done | bytes 786464 | tf_op jit(solution)/shard_map/cond/branch_1_fun/ppermute | solution.py:23
  98.8 2.6 copy.46
  101.5 14.1 %collective-permute-done.7 = bf16[1,192,2048]{2,1,0:T(8,128)(2,1)} collective-permute-done((bf16[1,192,2048]{2,1,0:T(8,128)(2,1)}, bf16[1,192,2048]{2,1,0:T(8,128)(2,1)}, u32[]{:S(2)}, u32[]{:S(2)}) %collective-permute-start.7) | collective-permute-done | bytes 786464 | tf_op jit(solution)/shard_map/cond/branch_1_fun/ppermute | solution.py:23
  115.6 2.2 copy.47
  117.9 2.7 %collective-permute-done.18 = bf16[256,2176]{1,0:T(8,128)(2,1)S(1)} collective-permute-done((bf16[256,2176]{1,0:T(8,128)(2,1)S(1)}, bf16[256,2176]{1,0:T(8,128)(2,1)S(1)}, u32[]{:S(2)}, u32[]{:S(2)}) %collective-permute-start.18) | collective-permute-done | bytes 1114144 | tf_op jit(solution)/shard_map/ppermute | solution.py:23
  120.6 39.9 %conditional.7 = (bf16[1,256,2,768]{3,2,1,0:T(2,128)(2,1)}, bf16[1,256,2,768]{3,2,1,0:T(2,128)(2,1)}, bf16[1,192,2048]{2,1,0:T(8,128)(2,1)}, bf16[1,256,2,768]{3...) conditional(s32[]{:T(128)} %bitcast.6, (s32[]{:T(128)}, ...), branch_computations={%region_8.10_spmd, %region_10.12_spmd} | conditional | flops 4835639808 | bytes 63839124 | solution.py:186
  120.6 3.4 %collective-permute-start.9 = (bf16[1,256,2,768]{3,2,1,0:T(2,128)(2,1)}, bf16[1,256,2,768]{3,2,1,0:T(2,128)(2,1)}, u32[]{:S(2)}, u32[]{:S(2)}) collective-permute-start(bf16[1,256,2,768]{3,2,1,0:T(2,128)(2,1)} %get-tuple-element.177), channel_id=1, source_target_pairs={{0,8},{1,9},{2,10},{3,11},{4,12},{5,13},{6,14},{7,15},{8,0},{9,1},... | collective-permute-start | bytes 2359304 | tf_op jit(solution)/shard_map/cond/branch_1_fun/ppermute | solution.py:23
  124.0 1.5 collective-permute-start.10
  126.3 5.7 %fusion.25 = f32[512,1536]{1,0:T(8,128)S(1)} fusion(bf16[2048,1536]{1,0:T(8,128)(2,1)} %get-tuple-element.185, bf16[512,2176]{1,0:T(8,128)(2,1)S(1)} %constant_dynamic-update-slice_fusion.6), kind=kOutput, calls=%fused_computation.65 | convolution fusion | flops 3221225472 | bytes 11534336 | tf_op jit(solution)/shard_map/cond/branch_1_fun/dot_general | solution.py:33
  132.1 1.8 convolution_multiply_fusion.3
  134.0 1.1 slice.183
  135.1 1.5 slice.125
  136.6 1.8 constant_dynamic-slice_fusion.9
  138.4 11.1 %collective-permute-done.9 = bf16[1,256,2,768]{3,2,1,0:T(2,128)(2,1)} collective-permute-done((bf16[1,256,2,768]{3,2,1,0:T(2,128)(2,1)}, bf16[1,256,2,768]{3,2,1,0:T(2,128)(2,1)}, u32[]{:S(2)}, u32[]{:S(2)}) %collective-permute-start.9) | collective-permute-done | bytes 786464 | tf_op jit(solution)/shard_map/cond/branch_1_fun/ppermute | solution.py:23
  149.5 2.6 copy.59
  152.1 8.4 %collective-permute-done.11 = bf16[1,192,2048]{2,1,0:T(8,128)(2,1)} collective-permute-done((bf16[1,192,2048]{2,1,0:T(8,128)(2,1)}, bf16[1,192,2048]{2,1,0:T(8,128)(2,1)}, u32[]{:S(2)}, u32[]{:S(2)}) %collective-permute-start.11) | collective-permute-done | bytes 786464 | tf_op jit(solution)/shard_map/cond/branch_1_fun/ppermute | solution.py:179
  161.0 3.6 %collective-permute-done.19 = bf16[256,2048]{1,0:T(8,128)(2,1)S(1)} collective-permute-done((bf16[256,2048]{1,0:T(8,128)(2,1)S(1)}, bf16[256,2048]{1,0:T(8,128)(2,1)S(1)}, u32[]{:S(2)}, u32[]{:S(2)}) %collective-permute-start.19) | collective-permute-done | bytes 1048608 | tf_op jit(solution)/shard_map/ppermute | solution.py:23
  164.6 2.9 %add_convert_fusion = bf16[256,2048]{1,0:T(8,128)(2,1)} fusion(f32[256,2048]{1,0:T(8,128)} %get-tuple-element.270, bf16[256,2048]{1,0:T(8,128)(2,1)S(1)} %collective-permute-done.19), kind=kLoop, calls=%fused_computation.85 | loop fusion | flops 1572864 | bytes 4194304 | tf_op jit(solution)/shard_map/convert_element_type | solution.py:251
  167.5 43.8 %conditional.8 = (bf16[1,256,2,768]{3,2,1,0:T(2,128)(2,1)S(1)}, bf16[1,192,2048]{2,1,0:T(8,128)(2,1)S(1)}, bf16[1,256,2,768]{3,2,1,0:T(2,128)(2,1)}, f32[256,2048]{1,0:T(8,128)S(1)}) conditional(s32[]{:T(128)} %bitcast.6, (bf16[256,2048]{1,0:T(8,128)(2,1)S(1)}, f32[256,2048]{1,0:T(8,128)}, bf16[1,256,2,768]{3,2,1,0:T(2,128)(2,1)S(1)}, ...), branch_computations={%region_12.13_spmd, %region_13.14_spmd} | conditional | flops 1048576 | bytes 17825944 | solution.py:186
  167.9 2.6 %collective-permute-start.4 = (bf16[1,192,2048]{2,1,0:T(8,128)(2,1)S(1)}, bf16[1,192,2048]{2,1,0:T(8,128)(2,1)S(1)}, u32[]{:S(2)}, u32[]{:S(2)}) collective-permute-start(bf16[1,192,2048]{2,1,0:T(8,128)(2,1)S(1)} %get-tuple-element.196), channel_id=1, source_target_pairs={{0,8},{1,9},{2,10},{3,11},{4,12},{5,13},{6,14},{7,15},{8,0},{9,1},... | collective-permute-start | bytes 2359304 | tf_op jit(solution)/shard_map/cond/branch_1_fun/ppermute | solution.py:23
  170.5 1.5 collective-permute-start.5
  172.0 1.9 convert_add_fusion.1
  173.9 20.6 %collective-permute-done.3 = bf16[1,256,2,768]{3,2,1,0:T(2,128)(2,1)S(1)} collective-permute-done((bf16[1,256,2,768]{3,2,1,0:T(2,128)(2,1)S(1)}, bf16[1,256,2,768]{3,2,1,0:T(2,128)(2,1)S(1)}, u32[]{:S(2)}, u32[]{:S(2)}) %collective-permute-start.3) | collective-permute-done | bytes 786464 | tf_op jit(solution)/shard_map/cond/branch_1_fun/ppermute | solution.py:23
  195.0 16.2 %collective-permute-done.4 = bf16[1,192,2048]{2,1,0:T(8,128)(2,1)S(1)} collective-permute-done((bf16[1,192,2048]{2,1,0:T(8,128)(2,1)S(1)}, bf16[1,192,2048]{2,1,0:T(8,128)(2,1)S(1)}, u32[]{:S(2)}, u32[]{:S(2)}) %collective-permute-start.4) | collective-permute-done | bytes 786464 | tf_op jit(solution)/shard_map/cond/branch_1_fun/ppermute | solution.py:23
  211.4 1.3 copy-done.6
  213.2 3.8 %fusion.37 = (bf16[256,2048]{1,0:T(8,128)(2,1)S(1)}, f32[256,2048]{1,0:T(8,128)}) fusion(f32[256,2048]{1,0:T(8,128)} %copy-done.6, bf16[256,2048]{1,0:T(8,128)(2,1)} %collective-permute-done.20), kind=kLoop, calls=%fused_computation.106 | loop fusion | flops 1572864 | bytes 6291456 | tf_op jit(solution)/shard_map/convert.7
  217.0 0.9 fusion.38
  217.9 2.0 collective-permute-start.23
  219.9 5.2 %collective-permute-start.22 = (bf16[64,2048]{1,0:T(8,128)(2,1)}, bf16[64,2048]{1,0:T(8,128)(2,1)}, u32[]{:S(2)}, u32[]{:S(2)}) collective-permute-start(bf16[64,2048]{1,0:T(8,128)(2,1)} %get-tuple-element.300), channel_id=1, source_target_pairs={{0,8},{1,9},{2,10},{3,11},{4,12},{5,13},{6,14},{7,15},{8,0},{9,1},... | collective-permute-start | bytes 786440 | tf_op jit(solution)/shard_map/ppermute | solution.py:257
  225.1 37.0 %conditional.9 = ((bf16[1,2048,2,768]{3,2,1,0:T(2,128)(2,1)}, bf16[1,768,2048]{2,1,0:T(8,128)(2,1)})) conditional(s32[]{:T(128)} %bitcast.6, (s32[]{:T(128)}, bf16[1,2048,2,768]{3,2,1,0:T(2,128)(2,1)S(1)}, bf16[1,768,2048]{2,1,0:T(8,128)(2,1)S(1)}) %tuple.91, (s32[]{:T(128)}, bf16[1,256,2,768]{3,2,1,0:T(2,128)(2,1)}, ...), branch_computations={%region_14.15_spmd, %region_15.16_spmd} | conditional | bytes 25165912 | solution.py:222
  225.1 1.5 collective-permute-start
  227.1 6.3 %branch_1_fun.2 = (bf16[1,2048,2,768]{3,2,1,0:T(2,128)(2,1)}, bf16[1,768,2048]{2,1,0:T(8,128)(2,1)}) custom-call(s32[1]{0:T(128)} %bitcast.5.group_ref, bf16[1,256,2,768]{3,2,1,0:T(2,128)(2,1)} %get-tuple-element.206.refs_0_, bf16[1,256,2,768]{3,2,1,0:T(2,128)(2,1)} %get-tuple-element.207.refs_1_, bf16[1,192,2048]{2,1,0:T(8,128)(2,1)} %get-tuple-element.208.refs_2_, ...), custom_call_target="tpu_custom_call" | custom-call | bytes 15728640 | tf_op jit(solution)/shard_map/cond/branch_1_fun/pallas_call | solution.py:131
  233.4 12.4 %collective-permute-done.refs_0_ = bf16[1,256,2,768]{3,2,1,0:T(2,128)(2,1)S(1)} collective-permute-done((bf16[1,256,2,768]{3,2,1,0:T(2,128)(2,1)}, bf16[1,256,2,768]{3,2,1,0:T(2,128)(2,1)S(1)}, u32[]{:S(2)}, u32[]{:S(2)}) %collective-permute-start) | collective-permute-done | bytes 786464 | tf_op jit(solution)/shard_map/cond/branch_1_fun/ppermute | solution.py:204
  245.8 15.0 %collective-permute-done.1.refs_1_ = bf16[1,192,2048]{2,1,0:T(8,128)(2,1)S(1)} collective-permute-done((bf16[1,192,2048]{2,1,0:T(8,128)(2,1)}, bf16[1,192,2048]{2,1,0:T(8,128)(2,1)S(1)}, u32[]{:S(2)}, u32[]{:S(2)}) %collective-permute-start.1) | collective-permute-done | bytes 786464 | tf_op jit(solution)/shard_map/cond/branch_1_fun/ppermute | solution.py:204
  260.8 1.3 branch_1_fun.3
  262.1 1.3 fusion.34
  (64 shorter events, 5.8 us)
Async XLA Ops:
  0.6 12.7 %copy-start.11 = (s32[8]{0:T(128)S(1)}, s32[8]{0:T(128)}, u32[]{:S(2)}) copy-start(s32[8]{0:T(128)} %param.27) | copy-start | bytes 100
  5.2 52.9 %collective-permute-start.14 = (bf16[64,2176]{1,0:T(8,128)(2,1)S(1)}, bf16[64,2176]{1,0:T(8,128)(2,1)S(1)}, u32[]{:S(2)}, u32[]{:S(2)}) collective-permute-start(bf16[64,2176]{1,0:T(8,128)(2,1)S(1)} %concatenate.34), channel_id=1, source_target_pairs={{0,12},{1,13},{2,14},{3,15},{4,0},{5,1},{6,2},{7,3},{8,4},{9,5},{1... | collective-permute-start | bytes 835592 | tf_op jit(solution)/shard_map/ppermute | solution.py:238
  5.2 52.9 %collective-permute-start.13 = (bf16[64,2176]{1,0:T(8,128)(2,1)S(1)}, bf16[64,2176]{1,0:T(8,128)(2,1)S(1)}, u32[]{:S(2)}, u32[]{:S(2)}) collective-permute-start(bf16[64,2176]{1,0:T(8,128)(2,1)S(1)} %concatenate.34), channel_id=1, source_target_pairs={{0,8},{1,9},{2,10},{3,11},{4,12},{5,13},{6,14},{7,15},{8,0},{9,1},... | collective-permute-start | bytes 835592 | tf_op jit(solution)/shard_map/ppermute | solution.py:238
  8.3 49.9 %collective-permute-start.12 = (bf16[64,2176]{1,0:T(8,128)(2,1)S(1)}, bf16[64,2176]{1,0:T(8,128)(2,1)S(1)}, u32[]{:S(2)}, u32[]{:S(2)}) collective-permute-start(bf16[64,2176]{1,0:T(8,128)(2,1)S(1)} %concatenate.34), channel_id=1, source_target_pairs={{0,4},{1,5},{2,6},{3,7},{4,8},{5,9},{6,10},{7,11},{8,12},{9,13},{1... | collective-permute-start | bytes 835592 | tf_op jit(solution)/shard_map/ppermute | solution.py:238
  14.6 42.7 %collective-permute-start.2 = (bf16[1,256,2,768]{3,2,1,0:T(2,128)(2,1)}, bf16[1,256,2,768]{3,2,1,0:T(2,128)(2,1)S(1)}, u32[]{:S(2)}, u32[]{:S(2)}) collective-permute-start(bf16[1,256,2,768]{3,2,1,0:T(2,128)(2,1)} %get-tuple-element.140), channel_id=1, source_target_pairs={{0,8},{1,9},{2,10},{3,11},{4,12},{5,13},{6,14},{7,15},{8,0},{9,1},... | collective-permute-start | bytes 2359304 | tf_op jit(solution)/shard_map/cond/branch_1_fun/ppermute | solution.py:23
  61.1 3.0 %collective-permute-start.16 = (bf16[256,2176]{1,0:T(8,128)(2,1)}, bf16[256,2176]{1,0:T(8,128)(2,1)S(1)}, u32[]{:S(2)}, u32[]{:S(2)}) collective-permute-start(bf16[256,2176]{1,0:T(8,128)(2,1)} %constant_dynamic-update-slice_fusion.8), channel_id=1, source_target_pairs={{0,1},{1,0},{2,3},{3,2},{4,5},{5,4},{6,7},{7,6},{8,9},{9,8},{10,11... | collective-permute-start | bytes 3342344 | tf_op jit(solution)/shard_map/ppermute | solution.py:23
  61.1 56.7 %collective-permute-start.15 = (bf16[256,2176]{1,0:T(8,128)(2,1)}, bf16[256,2176]{1,0:T(8,128)(2,1)S(1)}, u32[]{:S(2)}, u32[]{:S(2)}) collective-permute-start(bf16[256,2176]{1,0:T(8,128)(2,1)} %constant_dynamic-update-slice_fusion.8), channel_id=1, source_target_pairs={{0,2},{1,3},{2,0},{3,1},{4,6},{5,7},{6,4},{7,5},{8,10},{9,11},{10,... | collective-permute-start | bytes 3342344 | tf_op jit(solution)/shard_map/ppermute | solution.py:23
  64.1 34.8 %collective-permute-start.6 = (bf16[1,256,2,768]{3,2,1,0:T(2,128)(2,1)}, bf16[1,256,2,768]{3,2,1,0:T(2,128)(2,1)}, u32[]{:S(2)}, u32[]{:S(2)}) collective-permute-start(bf16[1,256,2,768]{3,2,1,0:T(2,128)(2,1)} %get-tuple-element.156), channel_id=1, source_target_pairs={{0,8},{1,9},{2,10},{3,11},{4,12},{5,13},{6,14},{7,15},{8,0},{9,1},... | collective-permute-start | bytes 2359304 | tf_op jit(solution)/shard_map/cond/branch_1_fun/ppermute | solution.py:23
  67.3 48.3 %collective-permute-start.7 = (bf16[1,192,2048]{2,1,0:T(8,128)(2,1)}, bf16[1,192,2048]{2,1,0:T(8,128)(2,1)}, u32[]{:S(2)}, u32[]{:S(2)}) collective-permute-start(bf16[1,192,2048]{2,1,0:T(8,128)(2,1)} %get-tuple-element.157), channel_id=1, source_target_pairs={{0,8},{1,9},{2,10},{3,11},{4,12},{5,13},{6,14},{7,15},{8,0},{9,1},... | collective-permute-start | bytes 2359304 | tf_op jit(solution)/shard_map/cond/branch_1_fun/ppermute | solution.py:23
  67.4 50.4 %collective-permute-start.8 = (bf16[1,256,2,768]{3,2,1,0:T(2,128)(2,1)}, bf16[1,256,2,768]{3,2,1,0:T(2,128)(2,1)}, u32[]{:S(2)}, u32[]{:S(2)}) collective-permute-start(bf16[1,256,2,768]{3,2,1,0:T(2,128)(2,1)} %get-tuple-element.158), channel_id=1, source_target_pairs={{0,16},{16,0},{1,17},{17,1},{2,18},{18,2},{3,19},{19,3},{4,20},{20... | collective-permute-start | bytes 2359304 | tf_op jit(solution)/shard_map/cond/branch_1_fun/ppermute | solution.py:179
  70.4 5.8 %copy-start.3 = (bf16[1,768,2048]{2,1,0:T(8,128)(2,1)S(1)}, bf16[1,768,2048]{2,1,0:T(8,128)(2,1)}, u32[]{:S(2)}) copy-start(bf16[1,768,2048]{2,1,0:T(8,128)(2,1)} %get-tuple-element.164) | copy-start | bytes 9437188 | tf_op jit(solution)/shard_map/cond
  117.8 2.8 %copy-start.10 = (bf16[256,2048]{1,0:T(8,128)(2,1)}, bf16[256,2048]{1,0:T(8,128)(2,1)S(1)}, u32[]{:S(2)}) copy-start(bf16[256,2048]{1,0:T(8,128)(2,1)S(1)} %get-tuple-element.260) | copy-start | bytes 3145732
  117.8 2.8 %collective-permute-start.18 = (bf16[256,2176]{1,0:T(8,128)(2,1)S(1)}, bf16[256,2176]{1,0:T(8,128)(2,1)S(1)}, u32[]{:S(2)}, u32[]{:S(2)}) collective-permute-start(bf16[256,2176]{1,0:T(8,128)(2,1)S(1)} %collective-permute-done.15), channel_id=1, source_target_pairs={{0,1},{1,0},{2,3},{3,2},{4,5},{5,4},{6,7},{7,6},{8,9},{9,8},{10,11... | collective-permute-start | bytes 3342344 | tf_op jit(solution)/shard_map/ppermute | solution.py:23
  120.6 28.9 %collective-permute-start.9 = (bf16[1,256,2,768]{3,2,1,0:T(2,128)(2,1)}, bf16[1,256,2,768]{3,2,1,0:T(2,128)(2,1)}, u32[]{:S(2)}, u32[]{:S(2)}) collective-permute-start(bf16[1,256,2,768]{3,2,1,0:T(2,128)(2,1)} %get-tuple-element.177), channel_id=1, source_target_pairs={{0,8},{1,9},{2,10},{3,11},{4,12},{5,13},{6,14},{7,15},{8,0},{9,1},... | collective-permute-start | bytes 2359304 | tf_op jit(solution)/shard_map/cond/branch_1_fun/ppermute | solution.py:23
  124.0 28.1 %collective-permute-start.10 = (bf16[1,256,2,768]{3,2,1,0:T(2,128)(2,1)}, bf16[1,256,2,768]{3,2,1,0:T(2,128)(2,1)}, u32[]{:S(2)}, u32[]{:S(2)}) collective-permute-start(bf16[1,256,2,768]{3,2,1,0:T(2,128)(2,1)} %get-tuple-element.178), channel_id=1, source_target_pairs={{0,16},{16,0},{1,17},{17,1},{2,18},{18,2},{3,19},{19,3},{4,20},{20... | collective-permute-start | bytes 2359304 | tf_op jit(solution)/shard_map/cond/branch_1_fun/ppermute | solution.py:179
  125.5 35.0 %collective-permute-start.11 = (bf16[1,192,2048]{2,1,0:T(8,128)(2,1)}, bf16[1,192,2048]{2,1,0:T(8,128)(2,1)}, u32[]{:S(2)}, u32[]{:S(2)}) collective-permute-start(bf16[1,192,2048]{2,1,0:T(8,128)(2,1)} %get-tuple-element.179), channel_id=1, source_target_pairs={{0,16},{16,0},{1,17},{17,1},{2,18},{18,2},{3,19},{19,3},{4,20},{20... | collective-permute-start | bytes 2359304 | tf_op jit(solution)/shard_map/cond/branch_1_fun/ppermute | solution.py:179
  126.3 5.8 %copy-start.5 = (bf16[1,768,2048]{2,1,0:T(8,128)(2,1)S(1)}, bf16[1,768,2048]{2,1,0:T(8,128)(2,1)}, u32[]{:S(2)}) copy-start(bf16[1,768,2048]{2,1,0:T(8,128)(2,1)} %get-tuple-element.182) | copy-start | bytes 9437188 | tf_op jit(solution)/shard_map/cond
  136.6 23.9 %copy-start.9 = (bf16[256,2048]{1,0:T(8,128)(2,1)S(1)}, bf16[256,2048]{1,0:T(8,128)(2,1)}, u32[]{:S(2)}) copy-start(bf16[256,2048]{1,0:T(8,128)(2,1)} %slice.183) | copy-start | bytes 3145732 | tf_op jit(solution)/shard_map/cond
  160.5 4.1 %collective-permute-start.19 = (bf16[256,2048]{1,0:T(8,128)(2,1)S(1)}, bf16[256,2048]{1,0:T(8,128)(2,1)S(1)}, u32[]{:S(2)}, u32[]{:S(2)}) collective-permute-start(bf16[256,2048]{1,0:T(8,128)(2,1)S(1)} %get-tuple-element.271), channel_id=1, source_target_pairs={{0,1},{1,0},{2,3},{3,2},{4,5},{5,4},{6,7},{7,6},{8,9},{9,8},{10,11... | collective-permute-start | bytes 3145736 | tf_op jit(solution)/shard_map/ppermute | solution.py:23
  160.5 7.0 %collective-permute-start.17 = (bf16[256,2048]{1,0:T(8,128)(2,1)}, bf16[256,2048]{1,0:T(8,128)(2,1)S(1)}, u32[]{:S(2)}, u32[]{:S(2)}) collective-permute-start(bf16[256,2048]{1,0:T(8,128)(2,1)} %copy-done.10), channel_id=1, source_target_pairs={{0,1},{1,0},{2,3},{3,2},{4,5},{5,4},{6,7},{7,6},{8,9},{9,8},{10,11... | collective-permute-start | bytes 3145736 | tf_op jit(solution)/shard_map/ppermute | solution.py:23
  167.5 43.9 %collective-permute-start.20 = (bf16[256,2048]{1,0:T(8,128)(2,1)}, bf16[256,2048]{1,0:T(8,128)(2,1)}, u32[]{:S(2)}, u32[]{:S(2)}) collective-permute-start(bf16[256,2048]{1,0:T(8,128)(2,1)} %add_convert_fusion), channel_id=1, source_target_pairs={{0,2},{1,3},{2,0},{3,1},{4,6},{5,7},{6,4},{7,5},{8,10},{9,11},{10,... | collective-permute-start | bytes 3145736 | tf_op jit(solution)/shard_map/ppermute | solution.py:23
  167.5 57.6 %copy-start.1 = (bf16[1,768,2048]{2,1,0:T(8,128)(2,1)S(1)}, bf16[1,768,2048]{2,1,0:T(8,128)(2,1)}, u32[]{:S(2)}) copy-start(bf16[1,768,2048]{2,1,0:T(8,128)(2,1)} %param.29) | copy-start | bytes 9437188
  167.5 27.0 %collective-permute-start.3 = (bf16[1,256,2,768]{3,2,1,0:T(2,128)(2,1)S(1)}, bf16[1,256,2,768]{3,2,1,0:T(2,128)(2,1)S(1)}, u32[]{:S(2)}, u32[]{:S(2)}) collective-permute-start(bf16[1,256,2,768]{3,2,1,0:T(2,128)(2,1)S(1)} %get-tuple-element.195), channel_id=1, source_target_pairs={{0,8},{1,9},{2,10},{3,11},{4,12},{5,13},{6,14},{7,15},{8,0},{9,1},... | collective-permute-start | bytes 2359304 | tf_op jit(solution)/shard_map/cond/branch_1_fun/ppermute | solution.py:23
  167.9 43.4 %collective-permute-start.4 = (bf16[1,192,2048]{2,1,0:T(8,128)(2,1)S(1)}, bf16[1,192,2048]{2,1,0:T(8,128)(2,1)S(1)}, u32[]{:S(2)}, u32[]{:S(2)}) collective-permute-start(bf16[1,192,2048]{2,1,0:T(8,128)(2,1)S(1)} %get-tuple-element.196), channel_id=1, source_target_pairs={{0,8},{1,9},{2,10},{3,11},{4,12},{5,13},{6,14},{7,15},{8,0},{9,1},... | collective-permute-start | bytes 2359304 | tf_op jit(solution)/shard_map/cond/branch_1_fun/ppermute | solution.py:23
  170.5 40.8 %collective-permute-start.5 = (bf16[1,256,2,768]{3,2,1,0:T(2,128)(2,1)}, bf16[1,256,2,768]{3,2,1,0:T(2,128)(2,1)}, u32[]{:S(2)}, u32[]{:S(2)}) collective-permute-start(bf16[1,256,2,768]{3,2,1,0:T(2,128)(2,1)} %get-tuple-element.197), channel_id=1, source_target_pairs={{0,16},{16,0},{1,17},{17,1},{2,18},{18,2},{3,19},{19,3},{4,20},{20... | collective-permute-start | bytes 2359304 | tf_op jit(solution)/shard_map/cond/branch_1_fun/ppermute | solution.py:179
  211.3 1.3 copy-start.6
  211.3 1.6 copy-start.7
  211.3 1.8 copy-start.8
  213.2 11.9 %copy-start = (bf16[1,2048,2,768]{3,2,1,0:T(2,128)(2,1)S(1)}, bf16[1,2048,2,768]{3,2,1,0:T(2,128)(2,1)}, u32[]{:S(2)}) copy-start(bf16[1,2048,2,768]{3,2,1,0:T(2,128)(2,1)} %param.28) | copy-start | bytes 18874372
  217.9 44.2 %collective-permute-start.21 = (bf16[64,2048]{1,0:T(8,128)(2,1)}, bf16[64,2048]{1,0:T(8,128)(2,1)S(1)}, u32[]{:S(2)}, u32[]{:S(2)}) collective-permute-start(bf16[64,2048]{1,0:T(8,128)(2,1)} %get-tuple-element.298), channel_id=1, source_target_pairs={{0,12},{1,13},{2,14},{3,15},{4,0},{5,1},{6,2},{7,3},{8,4},{9,5},{1... | collective-permute-start | bytes 786440 | tf_op jit(solution)/shard_map/ppermute | solution.py:257
  217.9 44.2 %collective-permute-start.23 = (bf16[64,2048]{1,0:T(8,128)(2,1)}, bf16[64,2048]{1,0:T(8,128)(2,1)}, u32[]{:S(2)}, u32[]{:S(2)}) collective-permute-start(bf16[64,2048]{1,0:T(8,128)(2,1)} %get-tuple-element.299), channel_id=1, source_target_pairs={{0,4},{1,5},{2,6},{3,7},{4,8},{5,9},{6,10},{7,11},{8,12},{9,13},{1... | collective-permute-start | bytes 786440 | tf_op jit(solution)/shard_map/ppermute | solution.py:257
  219.9 42.2 %collective-permute-start.22 = (bf16[64,2048]{1,0:T(8,128)(2,1)}, bf16[64,2048]{1,0:T(8,128)(2,1)}, u32[]{:S(2)}, u32[]{:S(2)}) collective-permute-start(bf16[64,2048]{1,0:T(8,128)(2,1)} %get-tuple-element.300), channel_id=1, source_target_pairs={{0,8},{1,9},{2,10},{3,11},{4,12},{5,13},{6,14},{7,15},{8,0},{9,1},... | collective-permute-start | bytes 786440 | tf_op jit(solution)/shard_map/ppermute | solution.py:257
  225.1 20.7 %collective-permute-start = (bf16[1,256,2,768]{3,2,1,0:T(2,128)(2,1)}, bf16[1,256,2,768]{3,2,1,0:T(2,128)(2,1)S(1)}, u32[]{:S(2)}, u32[]{:S(2)}) collective-permute-start(bf16[1,256,2,768]{3,2,1,0:T(2,128)(2,1)} %get-tuple-element.204.refs_4_), channel_id=1, source_target_pairs={{0,16},{16,0},{1,17},{17,1},{2,18},{18,2},{3,19},{19,3},{4,20},{20... | collective-permute-start | bytes 2359304 | tf_op jit(solution)/shard_map/cond/branch_1_fun/ppermute | solution.py:204
  226.6 34.2 %collective-permute-start.1 = (bf16[1,192,2048]{2,1,0:T(8,128)(2,1)}, bf16[1,192,2048]{2,1,0:T(8,128)(2,1)S(1)}, u32[]{:S(2)}, u32[]{:S(2)}) collective-permute-start(bf16[1,192,2048]{2,1,0:T(8,128)(2,1)} %get-tuple-element.205.refs_5_), channel_id=1, source_target_pairs={{0,16},{16,0},{1,17},{17,1},{2,18},{18,2},{3,19},{19,3},{4,20},{20... | collective-permute-start | bytes 2359304 | tf_op jit(solution)/shard_map/cond/branch_1_fun/ppermute | solution.py:204
